TPU v7x, 512 devices: a whole 4x4x16 slice. The times are simulated.
512 devices in a mesh: leaf: 64 (over x, z), blk: 8 (over y, core).
Axes of the slice: x: 4, y: 4, z: 16, core: 2. Of those that a mesh axis runs over, the one named last changes fastest.
Arguments:
- leaf_inverse: bfloat16 [64, 1024, 1024], P('leaf', 'blk'), as said below
- leaf_coupling: bfloat16 [64, 6, 1024, 1024], P('leaf', None, None, 'blk'), as said below
- sep_inverse: bfloat16 [64, 1024, 1024], P('leaf', 'blk'), as said below
- sep_coupling: bfloat16 [64, 6, 1024, 1024], P('leaf', None, None, 'blk'), as said below
- leaf_right: bfloat16 [64, 64, 1024], P('leaf', None, 'blk'), may hold values from -6 to 6
- sep_right: bfloat16 [64, 64, 1024], P('leaf', None, 'blk'), may hold values from -6 to 6
- pattern: int32 [64, 6], P('leaf'), may hold values 0 or 1
Outputs:
- leaf_sol: float32 [64, 64, 1024], P('leaf', None, 'blk')
- sep_sol: float32 [64, 64, 1024], P('leaf', None, 'blk')
Inputs may be any that keep to these rules, and one draw needn't show every extreme that they name: `leaf_inverse`: inverses of the leaves' diagonal blocks. `leaf_coupling`: off-diagonal factor blocks of the leaves. `sep_inverse`: inverses of the separators' diagonal blocks. `sep_coupling`: off-diagonal factor blocks of the separators.
All inputs are finite; a program needn't handle non-finite values. No bound on the sum of `pattern` on one device may be relied on, other than what follows from the above.
Results may differ from a plain program's by a relative error of at most 0.02.
Values may be sent and summed in bfloat16 or wider, within the bound.
A program may use at most 64 MiB of HBM per device.

v0:
```python
import jax
import jax.numpy as jnp
from jax import lax
from jax.sharding import PartitionSpec as P


def swapped(block, axis, stride):
    count = lax.axis_size(axis)
    route = []
    for low in range(count):
        high = low | 1 << stride
        if high != low and high < count:
            route += [(low, high), (high, low)]
    return lax.ppermute(block, axis, route)


def group_total(partial_sum, height):
    summed = partial_sum
    for bit_pos in range(height):
        summed = summed + swapped(summed, "leaf", bit_pos)
    return lax.psum(summed, "blk")


def body(leaf_inverse, leaf_coupling, sep_inverse, sep_coupling, leaf_right, sep_right, pattern):
    levels = leaf_coupling.shape[1]
    rhs_count = leaf_right.shape[1]
    sep_rows = sep_inverse.shape[2]
    own_width = sep_right.shape[2]
    contract_rows = (((1,), (1,)), ((), ()))
    mask_f = pattern[0].astype(jnp.float32)
    leaf_index = lax.axis_index("leaf")
    blk_index = lax.axis_index("blk")
    own_level = jnp.int32(1)
    running = jnp.int32(1)
    for bit_pos in range(levels):
        running = running * (leaf_index >> bit_pos & 1)
        own_level = own_level + running
    leaf_full, sep_full = (
        lax.all_gather(leaf_right[0], "blk", axis=1, tiled=True),
        lax.all_gather(sep_right[0], "blk", axis=1, tiled=True),
    )
    leaf_y = lax.dot_general(
        leaf_full, leaf_inverse[0], contract_rows, preferred_element_type=jnp.float32
    )
    leaf_terms = jnp.einsum(
        "rs,lps->lrp",
        leaf_y.astype(jnp.bfloat16),
        leaf_coupling[0],
        preferred_element_type=jnp.float32,
    )
    leaf_terms = leaf_terms * mask_f[:, None, None]
    sep_terms = jnp.zeros((levels, rhs_count, sep_rows), jnp.float32)
    own_solve = jnp.zeros((rhs_count, own_width), jnp.float32)
    for height in range(1, levels + 1):
        grand = group_total(leaf_terms[height - 1] + sep_terms[height - 1], height)
        residue = sep_full.astype(jnp.float32) - grand
        later = (jnp.arange(levels) >= height).astype(jnp.float32)[:, None, None]

        def solve_owned(residue_in, later=later):
            own_rows = lax.dot_general(
                residue_in.astype(jnp.bfloat16),
                sep_inverse[0],
                contract_rows,
                preferred_element_type=jnp.float32,
            )
            spread = jnp.einsum(
                "rq,lpq->lrp",
                own_rows.astype(jnp.bfloat16),
                sep_coupling[0],
                preferred_element_type=jnp.float32,
            )
            return (own_rows, spread * later)

        def skip_owned(residue_in):
            return (
                jnp.zeros((rhs_count, own_width), jnp.float32),
                jnp.zeros((levels, rhs_count, sep_rows), jnp.float32),
            )

        own_rows, spread = lax.cond(own_level == height, solve_owned, skip_owned, residue)
        own_solve = own_solve + own_rows
        sep_terms = sep_terms + spread
    ancestor = {}
    own_sol = jnp.zeros((rhs_count, own_width), jnp.float32)
    for height in range(levels, 0, -1):

        def back_owned(rows_in, height=height):
            for upper in range(height + 1, levels + 1):
                rows_in = rows_in - jnp.dot(
                    ancestor[upper], sep_coupling[0, upper - 1], preferred_element_type=jnp.float32
                )
            return jnp.dot(
                rows_in.astype(jnp.bfloat16), sep_inverse[0], preferred_element_type=jnp.float32
            )

        def back_skip(rows_in):
            return jnp.zeros((rhs_count, sep_rows), jnp.float32)

        partial_sum = lax.cond(own_level == height, back_owned, back_skip, own_solve)
        summed = group_total(partial_sum, height)
        ancestor[height] = summed.astype(jnp.bfloat16)
        row_piece = lax.dynamic_slice_in_dim(summed, blk_index * own_width, own_width, 1)
        own_sol = jnp.where(own_level == height, row_piece, own_sol)
    residual_rows = leaf_y
    for upper in range(1, levels + 1):
        residual_rows = residual_rows - mask_f[upper - 1] * jnp.dot(
            ancestor[upper], leaf_coupling[0, upper - 1], preferred_element_type=jnp.float32
        )
    spread_back = jnp.dot(
        residual_rows.astype(jnp.bfloat16), leaf_inverse[0], preferred_element_type=jnp.float32
    )
    leaf_sol = lax.psum_scatter(
        spread_back.astype(jnp.bfloat16), "blk", scatter_dimension=1, tiled=True
    ).astype(jnp.float32)
    return (leaf_sol[None], own_sol[None])


def solution(mesh):
    in_specs = (
        P("leaf", "blk", None),
        P("leaf", None, None, "blk"),
        P("leaf", "blk", None),
        P("leaf", None, None, "blk"),
        P("leaf", None, "blk"),
        P("leaf", None, "blk"),
        P("leaf", None),
    )
    out_specs = (P("leaf", None, "blk"), P("leaf", None, "blk"))
    return jax.shard_map(body, mesh=mesh, in_specs=in_specs, out_specs=out_specs, check_vma=False)
```

profile of v0, /device:TPU:1, one launch (start us, length us, event | category | flops | bytes accessed | tf_op | source)
XLA Modules:
  0.0 1770.2 jit_solution(2177585648633450541)
XLA Ops:
  7.2 18.4 %all-gather = bf16[1,64,1024]{2,1,0:T(8,128)(2,1)S(1)} all-gather(bf16[1,64,128]{2,1,0:T(8,128)(2,1)} %param.35), channel_id=2, replica_groups=mesh['leaf'=64,'blk'=8] {'blk'}, dimensions={2}, use_global_device_ids=true | all-gather | bytes 147456 | tf_op jit(solution)/shard_map/all_gather | solution.py:39
  30.8 11.3 all-gather.1
  43.1 73.5 %all-reduce.13.cloned.1.call-done = f32[64,1024]{1,0:T(8,128)} async-done(((f32[64,1024]{1,0:T(8,128)}), f32[64,1024]{1,0:T(8,128)}) %all-reduce.13.cloned.1.call-update) | async-done | bytes 262160 | tf_op jit(solution)/shard_map/psum | solution.py:21
  133.6 13.1 collective-permute-done.2
  147.5 77.6 %all-reduce.15.cloned.1.call-done = f32[64,1024]{1,0:T(8,128)} async-done(((f32[64,1024]{1,0:T(8,128)}), f32[64,1024]{1,0:T(8,128)}) %all-reduce.15.cloned.1.call-update) | async-done | bytes 262160 | tf_op jit(solution)/shard_map/psum | solution.py:21
  242.1 13.4 collective-permute-done.4
  255.6 7.4 collective-permute-start.5
  263.0 21.5 %collective-permute-done.5 = f32[64,1024]{1,0:T(8,128)S(1)} collective-permute-done((f32[64,1024]{1,0:T(8,128)S(1)}, f32[64,1024]{1,0:T(8,128)S(1)}, u32[]{:S(2)}, u32[]{:S(2)}) %collective-permute-start.5) | collective-permute-done | bytes 262176 | tf_op jit(solution)/shard_map/ppermute | solution.py:14
  285.3 78.8 %all-reduce.17.cloned.1.call-done = f32[64,1024]{1,0:T(8,128)} async-done(((f32[64,1024]{1,0:T(8,128)}), f32[64,1024]{1,0:T(8,128)}) %all-reduce.17.cloned.1.call-update) | async-done | bytes 262160 | tf_op jit(solution)/shard_map/psum | solution.py:21
  382.3 11.1 collective-permute-done.7
  398.4 24.9 %collective-permute-done.8 = f32[64,1024]{1,0:T(8,128)S(1)} collective-permute-done((f32[64,1024]{1,0:T(8,128)S(1)}, f32[64,1024]{1,0:T(8,128)S(1)}, u32[]{:S(2)}, u32[]{:S(2)}) %collective-permute-start.8) | collective-permute-done | bytes 262176 | tf_op jit(solution)/shard_map/ppermute | solution.py:14
  423.4 15.8 collective-permute-start.9
  439.1 12.5 collective-permute-done.9
  452.5 77.7 %all-reduce.19.cloned.1.call-done = f32[64,1024]{1,0:T(8,128)} async-done(((f32[64,1024]{1,0:T(8,128)}), f32[64,1024]{1,0:T(8,128)}) %all-reduce.19.cloned.1.call-update) | async-done | bytes 262160 | tf_op jit(solution)/shard_map/psum | solution.py:21
  546.2 12.7 collective-permute-done.11
  559.0 8.0 collective-permute-start.12
  567.0 22.6 %collective-permute-done.12 = f32[64,1024]{1,0:T(8,128)S(1)} collective-permute-done((f32[64,1024]{1,0:T(8,128)S(1)}, f32[64,1024]{1,0:T(8,128)S(1)}, u32[]{:S(2)}, u32[]{:S(2)}) %collective-permute-start.12) | collective-permute-done | bytes 262176 | tf_op jit(solution)/shard_map/ppermute | solution.py:14
  589.6 8.5 collective-permute-start.13
  598.2 21.4 %collective-permute-done.13 = f32[64,1024]{1,0:T(8,128)S(1)} collective-permute-done((f32[64,1024]{1,0:T(8,128)S(1)}, f32[64,1024]{1,0:T(8,128)S(1)}, u32[]{:S(2)}, u32[]{:S(2)}) %collective-permute-start.13) | collective-permute-done | bytes 262176 | tf_op jit(solution)/shard_map/ppermute | solution.py:14
  629.5 76.0 %all-reduce.21.cloned.1.call-done = f32[64,1024]{1,0:T(8,128)} async-done(((f32[64,1024]{1,0:T(8,128)}), f32[64,1024]{1,0:T(8,128)}) %all-reduce.21.cloned.1.call-update) | async-done | bytes 262160 | tf_op jit(solution)/shard_map/psum | solution.py:21
  718.1 12.7 collective-permute-done.16
  736.5 23.6 %collective-permute-done.17 = f32[64,1024]{1,0:T(8,128)S(1)} collective-permute-done((f32[64,1024]{1,0:T(8,128)S(1)}, f32[64,1024]{1,0:T(8,128)S(1)}, u32[]{:S(2)}, u32[]{:S(2)}) %collective-permute-start.17) | collective-permute-done | bytes 262176 | tf_op jit(solution)/shard_map/ppermute | solution.py:14
  760.1 15.5 collective-permute-start.18
  775.6 12.7 collective-permute-done.18
  810.3 76.8 %all-reduce.23.cloned.1.call-done = f32[64,1024]{1,0:T(8,128)} async-done(((f32[64,1024]{1,0:T(8,128)}), f32[64,1024]{1,0:T(8,128)}) %all-reduce.23.cloned.1.call-update) | async-done | bytes 262160 | tf_op jit(solution)/shard_map/psum | solution.py:21
  898.7 12.7 collective-permute-done.22
  917.1 23.6 %collective-permute-done.23 = f32[64,1024]{1,0:T(8,128)S(1)} collective-permute-done((f32[64,1024]{1,0:T(8,128)S(1)}, f32[64,1024]{1,0:T(8,128)S(1)}, u32[]{:S(2)}, u32[]{:S(2)}) %collective-permute-start.23) | collective-permute-done | bytes 262176 | tf_op jit(solution)/shard_map/ppermute | solution.py:14
  940.7 15.5 collective-permute-start.24
  956.3 14.3 collective-permute-done.24
  990.6 76.1 %all-reduce.25.cloned.1.call-done = f32[64,1024]{1,0:T(8,128)} async-done(((f32[64,1024]{1,0:T(8,128)}), f32[64,1024]{1,0:T(8,128)}) %all-reduce.25.cloned.1.call-update) | async-done | bytes 262160 | tf_op jit(solution)/shard_map/psum | solution.py:21
  1078.4 12.7 collective-permute-done.28
  1096.8 23.6 %collective-permute-done.29 = f32[64,1024]{1,0:T(8,128)S(1)} collective-permute-done((f32[64,1024]{1,0:T(8,128)S(1)}, f32[64,1024]{1,0:T(8,128)S(1)}, u32[]{:S(2)}, u32[]{:S(2)}) %collective-permute-start.29) | collective-permute-done | bytes 262176 | tf_op jit(solution)/shard_map/ppermute | solution.py:14
  1120.4 15.5 collective-permute-start.30
  1136.0 14.8 collective-permute-done.30
  1153.4 6.6 collective-permute-done.31
  1160.9 74.7 %all-reduce.27.cloned.1.call-done = f32[64,1024]{1,0:T(8,128)} async-done(((f32[64,1024]{1,0:T(8,128)}), f32[64,1024]{1,0:T(8,128)}) %all-reduce.27.cloned.1.call-update) | async-done | bytes 262160 | tf_op jit(solution)/shard_map/psum | solution.py:21
  1247.3 12.7 collective-permute-done.33
  1266.1 23.7 %collective-permute-done.34 = f32[64,1024]{1,0:T(8,128)S(1)} collective-permute-done((f32[64,1024]{1,0:T(8,128)S(1)}, f32[64,1024]{1,0:T(8,128)S(1)}, u32[]{:S(2)}, u32[]{:S(2)}) %collective-permute-start.34) | collective-permute-done | bytes 262176 | tf_op jit(solution)/shard_map/ppermute | solution.py:14
  1289.9 15.0 collective-permute-start.35
  1304.8 14.4 collective-permute-done.35
  1320.0 74.0 %all-reduce.29.cloned.1.call-done = f32[64,1024]{1,0:T(8,128)} async-done(((f32[64,1024]{1,0:T(8,128)}), f32[64,1024]{1,0:T(8,128)}) %all-reduce.29.cloned.1.call-update) | async-done | bytes 262160 | tf_op jit(solution)/shard_map/psum | solution.py:21
  1406.5 12.3 collective-permute-done.37
  1424.4 24.2 %collective-permute-done.38 = f32[64,1024]{1,0:T(8,128)S(1)} collective-permute-done((f32[64,1024]{1,0:T(8,128)S(1)}, f32[64,1024]{1,0:T(8,128)S(1)}, u32[]{:S(2)}, u32[]{:S(2)}) %collective-permute-start.38) | collective-permute-done | bytes 262176 | tf_op jit(solution)/shard_map/ppermute | solution.py:14
  1449.4 77.1 %all-reduce.31.cloned.1.call-done = f32[64,1024]{1,0:T(8,128)} async-done(((f32[64,1024]{1,0:T(8,128)}), f32[64,1024]{1,0:T(8,128)}) %all-reduce.31.cloned.1.call-update) | async-done | bytes 262160 | tf_op jit(solution)/shard_map/psum | solution.py:21
  1538.3 11.9 collective-permute-done.40
  1551.0 78.9 %all-reduce.33.cloned.1.call-done = f32[64,1024]{1,0:T(8,128)} async-done(((f32[64,1024]{1,0:T(8,128)}), f32[64,1024]{1,0:T(8,128)}) %all-reduce.33.cloned.1.call-update) | async-done | bytes 262160 | tf_op jit(solution)/shard_map/psum | solution.py:21
  1641.1 76.8 %all-reduce.35.cloned.1.call-done = f32[64,1024]{1,0:T(8,128)} async-done(((f32[64,1024]{1,0:T(8,128)}), f32[64,1024]{1,0:T(8,128)}) %all-reduce.35.cloned.1.call-update) | async-done | bytes 262160 | tf_op jit(solution)/shard_map/psum | solution.py:21
  1726.3 35.9 %reduce-scatter.4.cloned.1.call-done = bf16[128,64]{1,0:T(8,128)(2,1)} async-done(((bf16[1024,64]{1,0:T(8,128)(2,1)}), bf16[128,64]{1,0:T(8,128)(2,1)}) %reduce-scatter.4.cloned.1.call-update) | async-done | bytes 16400
  (210 shorter events, 271.6 us)
Async XLA Ops:
  7.2 109.4 %all-reduce.13.cloned.1.call-start = ((), (), s32[]{:S(2)}) async-start(), calls=%async_computation.1 | async-start | bytes 524288 | tf_op jit(solution)/shard_map/psum | solution.py:21
  28.6 13.6 collective-permute-start
  42.9 182.2 %all-reduce.15.cloned.1.call-start = ((), (), s32[]{:S(2)}) async-start(), calls=%async_computation.2 | async-start | bytes 524288 | tf_op jit(solution)/shard_map/psum | solution.py:21
  130.5 16.2 collective-permute-start.2
  147.5 216.6 %all-reduce.17.cloned.1.call-start = ((), (), s32[]{:S(2)}) async-start(), calls=%async_computation.3 | async-start | bytes 524288 | tf_op jit(solution)/shard_map/psum | solution.py:21
  231.4 8.7 collective-permute-start.3
  240.2 15.4 collective-permute-start.4
  255.6 28.8 %collective-permute-start.5 = (f32[64,1024]{1,0:T(8,128)S(1)}, f32[64,1024]{1,0:T(8,128)S(1)}, u32[]{:S(2)}, u32[]{:S(2)}) collective-permute-start(f32[64,1024]{1,0:T(8,128)S(1)} %add.247), channel_id=1, source_target_pairs={{0,32},{32,0},{8,40},{40,8},{16,48},{48,16},{24,56},{56,24},{64,96... | collective-permute-start | bytes 786440 | tf_op jit(solution)/shard_map/ppermute | solution.py:14
  285.2 245.0 %all-reduce.19.cloned.1.call-start = ((), (), s32[]{:S(2)}) async-start(), calls=%async_computation.4 | async-start | bytes 524288 | tf_op jit(solution)/shard_map/psum | solution.py:21
  376.9 16.5 collective-permute-start.7
  393.5 29.9 %collective-permute-start.8 = (f32[64,1024]{1,0:T(8,128)S(1)}, f32[64,1024]{1,0:T(8,128)S(1)}, u32[]{:S(2)}, u32[]{:S(2)}) collective-permute-start(f32[64,1024]{1,0:T(8,128)S(1)} %add.254), channel_id=1, source_target_pairs={{0,32},{32,0},{8,40},{40,8},{16,48},{48,16},{24,56},{56,24},{64,96... | collective-permute-start | bytes 786440 | tf_op jit(solution)/shard_map/ppermute | solution.py:14
  423.4 28.3 %collective-permute-start.9 = (f32[64,1024]{1,0:T(8,128)S(1)}, f32[64,1024]{1,0:T(8,128)S(1)}, u32[]{:S(2)}, u32[]{:S(2)}) collective-permute-start(f32[64,1024]{1,0:T(8,128)S(1)} %add.255), channel_id=1, source_target_pairs={{0,64},{64,0},{8,72},{72,8},{16,80},{80,16},{24,88},{88,24},{32,96... | collective-permute-start | bytes 786440 | tf_op jit(solution)/shard_map/ppermute | solution.py:14
  452.5 253.0 %all-reduce.21.cloned.1.call-start = ((), (), s32[]{:S(2)}) async-start(), calls=%async_computation.5 | async-start | bytes 524288 | tf_op jit(solution)/shard_map/psum | solution.py:21
  543.1 15.9 collective-permute-start.11
  559.0 30.6 %collective-permute-start.12 = (f32[64,1024]{1,0:T(8,128)S(1)}, f32[64,1024]{1,0:T(8,128)S(1)}, u32[]{:S(2)}, u32[]{:S(2)}) collective-permute-start(f32[64,1024]{1,0:T(8,128)S(1)} %add.262), channel_id=1, source_target_pairs={{0,32},{32,0},{8,40},{40,8},{16,48},{48,16},{24,56},{56,24},{64,96... | collective-permute-start | bytes 786440 | tf_op jit(solution)/shard_map/ppermute | solution.py:14
  589.6 30.0 %collective-permute-start.13 = (f32[64,1024]{1,0:T(8,128)S(1)}, f32[64,1024]{1,0:T(8,128)S(1)}, u32[]{:S(2)}, u32[]{:S(2)}) collective-permute-start(f32[64,1024]{1,0:T(8,128)S(1)} %add.263), channel_id=1, source_target_pairs={{0,64},{64,0},{8,72},{72,8},{16,80},{80,16},{24,88},{88,24},{32,96... | collective-permute-start | bytes 786440 | tf_op jit(solution)/shard_map/ppermute | solution.py:14
  619.6 9.0 collective-permute-start.14
  629.4 257.7 %all-reduce.23.cloned.1.call-start = ((), (), s32[]{:S(2)}) async-start(), calls=%async_computation.6 | async-start | bytes 524288 | tf_op jit(solution)/shard_map/psum | solution.py:21
  707.4 7.5 collective-permute-start.15
  715.0 15.9 collective-permute-start.16
  730.9 29.2 %collective-permute-start.17 = (f32[64,1024]{1,0:T(8,128)S(1)}, f32[64,1024]{1,0:T(8,128)S(1)}, u32[]{:S(2)}, u32[]{:S(2)}) collective-permute-start(f32[64,1024]{1,0:T(8,128)S(1)} %add.271), channel_id=1, source_target_pairs={{0,32},{32,0},{8,40},{40,8},{16,48},{48,16},{24,56},{56,24},{64,96... | collective-permute-start | bytes 786440 | tf_op jit(solution)/shard_map/ppermute | solution.py:14
  760.1 28.3 %collective-permute-start.18 = (f32[64,1024]{1,0:T(8,128)S(1)}, f32[64,1024]{1,0:T(8,128)S(1)}, u32[]{:S(2)}, u32[]{:S(2)}) collective-permute-start(f32[64,1024]{1,0:T(8,128)S(1)} %add.272), channel_id=1, source_target_pairs={{0,64},{64,0},{8,72},{72,8},{16,80},{80,16},{24,88},{88,24},{32,96... | collective-permute-start | bytes 786440 | tf_op jit(solution)/shard_map/ppermute | solution.py:14
  788.4 10.9 collective-permute-start.19
  799.3 10.1 collective-permute-start.20
  810.3 256.4 %all-reduce.25.cloned.1.call-start = ((), (), s32[]{:S(2)}) async-start(), calls=%async_computation.7 | async-start | bytes 524288 | tf_op jit(solution)/shard_map/psum | solution.py:21
  895.6 15.9 collective-permute-start.22
  911.5 29.2 %collective-permute-start.23 = (f32[64,1024]{1,0:T(8,128)S(1)}, f32[64,1024]{1,0:T(8,128)S(1)}, u32[]{:S(2)}, u32[]{:S(2)}) collective-permute-start(f32[64,1024]{1,0:T(8,128)S(1)} %add.278), channel_id=1, source_target_pairs={{0,32},{32,0},{8,40},{40,8},{16,48},{48,16},{24,56},{56,24},{64,96... | collective-permute-start | bytes 786440 | tf_op jit(solution)/shard_map/ppermute | solution.py:14
  940.7 29.9 %collective-permute-start.24 = (f32[64,1024]{1,0:T(8,128)S(1)}, f32[64,1024]{1,0:T(8,128)S(1)}, u32[]{:S(2)}, u32[]{:S(2)}) collective-permute-start(f32[64,1024]{1,0:T(8,128)S(1)} %add.279), channel_id=1, source_target_pairs={{0,64},{64,0},{8,72},{72,8},{16,80},{80,16},{24,88},{88,24},{32,96... | collective-permute-start | bytes 786440 | tf_op jit(solution)/shard_map/ppermute | solution.py:14
  970.6 9.2 collective-permute-start.25
  979.9 9.8 collective-permute-start.26
  990.5 245.0 %all-reduce.27.cloned.1.call-start = ((), (), s32[]{:S(2)}) async-start(), calls=%async_computation.8 | async-start | bytes 524288 | tf_op jit(solution)/shard_map/psum | solution.py:21
  1075.3 15.9 collective-permute-start.28
  1091.2 29.2 %collective-permute-start.29 = (f32[64,1024]{1,0:T(8,128)S(1)}, f32[64,1024]{1,0:T(8,128)S(1)}, u32[]{:S(2)}, u32[]{:S(2)}) collective-permute-start(f32[64,1024]{1,0:T(8,128)S(1)} %add.284), channel_id=1, source_target_pairs={{0,32},{32,0},{8,40},{40,8},{16,48},{48,16},{24,56},{56,24},{64,96... | collective-permute-start | bytes 786440 | tf_op jit(solution)/shard_map/ppermute | solution.py:14
  1120.4 30.4 %collective-permute-start.30 = (f32[64,1024]{1,0:T(8,128)S(1)}, f32[64,1024]{1,0:T(8,128)S(1)}, u32[]{:S(2)}, u32[]{:S(2)}) collective-permute-start(f32[64,1024]{1,0:T(8,128)S(1)} %add.285), channel_id=1, source_target_pairs={{0,64},{64,0},{8,72},{72,8},{16,80},{80,16},{24,88},{88,24},{32,96... | collective-permute-start | bytes 786440 | tf_op jit(solution)/shard_map/ppermute | solution.py:14
  1150.8 9.2 collective-permute-start.31
  1160.8 233.2 %all-reduce.29.cloned.1.call-start = ((), (), s32[]{:S(2)}) async-start(), calls=%async_computation.9 | async-start | bytes 524288 | tf_op jit(solution)/shard_map/psum | solution.py:21
  1236.6 7.5 collective-permute-start.32
  1244.2 15.9 collective-permute-start.33
  1260.1 29.7 %collective-permute-start.34 = (f32[64,1024]{1,0:T(8,128)S(1)}, f32[64,1024]{1,0:T(8,128)S(1)}, u32[]{:S(2)}, u32[]{:S(2)}) collective-permute-start(f32[64,1024]{1,0:T(8,128)S(1)} %add.289), channel_id=1, source_target_pairs={{0,32},{32,0},{8,40},{40,8},{16,48},{48,16},{24,56},{56,24},{64,96... | collective-permute-start | bytes 786440 | tf_op jit(solution)/shard_map/ppermute | solution.py:14
  1289.9 29.3 %collective-permute-start.35 = (f32[64,1024]{1,0:T(8,128)S(1)}, f32[64,1024]{1,0:T(8,128)S(1)}, u32[]{:S(2)}, u32[]{:S(2)}) collective-permute-start(f32[64,1024]{1,0:T(8,128)S(1)} %add.290), channel_id=1, source_target_pairs={{0,64},{64,0},{8,72},{72,8},{16,80},{80,16},{24,88},{88,24},{32,96... | collective-permute-start | bytes 786440 | tf_op jit(solution)/shard_map/ppermute | solution.py:14
  1320.0 206.6 %all-reduce.31.cloned.1.call-start = ((), (), s32[]{:S(2)}) async-start(), calls=%async_computation.10 | async-start | bytes 524288 | tf_op jit(solution)/shard_map/psum | solution.py:21
  1402.9 16.0 collective-permute-start.37
  1418.9 29.8 %collective-permute-start.38 = (f32[64,1024]{1,0:T(8,128)S(1)}, f32[64,1024]{1,0:T(8,128)S(1)}, u32[]{:S(2)}, u32[]{:S(2)}) collective-permute-start(f32[64,1024]{1,0:T(8,128)S(1)} %add.293), channel_id=1, source_target_pairs={{0,32},{32,0},{8,40},{40,8},{16,48},{48,16},{24,56},{56,24},{64,96... | collective-permute-start | bytes 786440 | tf_op jit(solution)/shard_map/ppermute | solution.py:14
  1449.4 180.5 %all-reduce.33.cloned.1.call-start = ((), (), s32[]{:S(2)}) async-start(), calls=%async_computation.11 | async-start | bytes 524288 | tf_op jit(solution)/shard_map/psum | solution.py:21
  1534.8 15.4 collective-permute-start.40
  1550.9 167.0 %all-reduce.35.cloned.1.call-start = ((), (), s32[]{:S(2)}) async-start(), calls=%async_computation.12 | async-start | bytes 524288 | tf_op jit(solution)/shard_map/psum | solution.py:21
  1631.9 7.7 collective-permute-start.41
  1640.3 121.8 %reduce-scatter.4.cloned.1.call-start = ((), (), s32[]{:S(2)}) async-start(), calls=%async_computation.13 | async-start | bytes 294912
  (18 other events, 467.3 us)
Sparse Core Ops, SparseCore 0:
  43.1 73.4 all-reduce.12
  147.6 77.5 all-reduce.14
  285.3 78.6 all-reduce.16
  452.6 77.5 all-reduce.18
  629.6 75.8 all-reduce.20
  810.4 76.6 all-reduce.22
  990.6 75.9 all-reduce.24
  1161.0 74.5 all-reduce.26
  1320.1 73.9 all-reduce.28
  1449.5 76.9 all-reduce.30
  1551.0 78.7 all-reduce.32
  1640.5 77.3 all-reduce.34
  1724.9 37.2 reduce-scatter.3
where the time goes:
time: 1770 us
  waiting for transfers between devices  1450 us (82%)
  starting transfers between devices  223 us (13%)
  other arithmetic  30.4 us (2%)
  blocking collectives  29.7 us (2%)
    psum x12, waiting for transfers between devices, group_total(): return lax.psum(summed, 'blk')  918 us
    ppermute x42, waiting for transfers between devices, swapped(): return lax.ppermute(block, axis, route)  493 us
    ppermute x42, starting transfers between devices, swapped(): return lax.ppermute(block, axis, route)  223 us
    unnamed x14, waiting for transfers between devices  36.1 us
  transfers between devices with their start and end apart: 55, of which 54 were waited for; matrix products, arithmetic and copies ran while one was open for 0% of the time, Pallas kernels for 0%

commit v1 on v0

v1 whole, which is shorter than its diff:
```python
import jax
import jax.numpy as jnp
from jax import lax
from jax.experimental import pallas as pl
from jax.experimental.pallas import tpu as pltpu
from jax.sharding import PartitionSpec as P

MESH = pl.DeviceIdType.MESH
F32 = jnp.float32
BF16 = jnp.bfloat16
NB = 8
LEV = 6


def tree_place(i):
    lev, half, run = 1, 1, 1
    for n in range(LEV):
        run = run * ((i // 2**n) % 2)
        lev = lev + run
        half = half + run * 2**n
    return lev, half


def dot_t(a, b):
    return lax.dot_general(a, b, (((1,), (1,)), ((), ())), preferred_element_type=F32)


def kernel(li, lc, si, sc, lr_in, sr_in, pat, lsol, ssol,
           LR, LY, T1, TL, RSL, U, UO1, UO2, UX, RX, SR, SY, TC, TN, RSS, XF, PB, RSB, LB, RLB, SA, LA,
           s_lr, r_lr, s_t1, s_tl, r_tl, s_u1, s_u2, r_ux, r_rx, s_sr, r_sr, s_tc, s_tn, r_tn,
           s_xf, s_xo, r_xf, s_pb, r_pb, s_lb, r_lb):
    i = lax.axis_index("leaf")
    b = lax.axis_index("blk")
    lev, half = tree_place(i)
    odd = i % 2
    even_slot = i - odd
    pair_slot = i + 1 - 2 * odd
    pb = (i // (2 * half)) % 2
    parent = i + half - 2 * half * pb
    kid0 = i - half // 2
    kid1 = i + half // 2
    lev_next, _ = tree_place(i + 1)
    owner = lev <= LEV

    def send(src, dst, ssem, rsem, leaf, blk):
        pltpu.make_async_remote_copy(src_ref=src, dst_ref=dst, send_sem=ssem, recv_sem=rsem,
                                     device_id=(leaf, blk), device_id_type=MESH).start()

    def drain(ref, sem):
        pltpu.make_async_copy(ref, ref, sem).wait()

    def others(fn):
        def step(d, c):
            fn(d, (b + d) % NB)
            return c
        lax.fori_loop(1, NB, step, 0)

    def all_blk(fn):
        def step(d, c):
            fn((b + d) % NB)
            return c
        lax.fori_loop(0, NB, step, 0)

    def full(ref):
        return jnp.concatenate([ref[c] for c in range(NB)], axis=1)

    def spread(ref, value):
        for c in range(NB):
            ref[c] = value[:, c * 128:(c + 1) * 128].astype(BF16)

    def sum7(ref):
        total = ref[0].astype(F32)
        for d in range(1, NB - 1):
            total = total + ref[d].astype(F32)
        return total

    barrier = pltpu.get_barrier_semaphore()

    def greet(leaf, blk):
        pl.semaphore_signal(barrier, inc=1, device_id=(leaf, blk), device_id_type=MESH)

    pair_is_kin = (lev == 2) | ((lev == 1) & (pb == 0))
    others(lambda d, t: greet(i, t))

    @pl.when(~pair_is_kin)
    def _():
        all_blk(lambda t: greet(pair_slot, t))

    @pl.when(lev < LEV)
    def _():
        all_blk(lambda t: greet(parent, t))

    @pl.when((lev >= 2) & owner)
    def _():
        all_blk(lambda t: greet(kid0, t))
        all_blk(lambda t: greet(kid1, t))

    peers = (7 + jnp.where(pair_is_kin, 0, 8) + jnp.where(lev < LEV, 8, 0)
             + jnp.where((lev >= 2) & owner, 16, 0))
    pl.semaphore_wait(barrier, peers)

    LR[b] = lr_in[0]
    others(lambda d, t: send(LR.at[b], LR.at[b], s_lr, r_lr, i, t))
    drain(LR.at[pl.ds(0, 7)], r_lr)
    ly = dot_t(full(LR), li[0])
    LY[...] = ly
    LA[...] = ly
    lyb = ly.astype(BF16)

    spread(T1, dot_t(lyb, lc[0, 0]) * pat[0, 0].astype(F32))

    @pl.when(odd == 1)
    def _():
        all_blk(lambda t: send(T1.at[t], RX.at[NB + b], s_t1, r_rx, even_slot, t))

    @pl.when(odd == 0)
    def _():
        RX[b] = T1[b]
        others(lambda d, t: send(T1.at[t], RX.at[b], s_t1, r_rx, i, t))

    for a in range(2, LEV + 1):
        n = a - 2
        spread(TL.at[n], dot_t(lyb, lc[0, a - 1]) * pat[0, a - 1].astype(F32))
        others(lambda d, t, n=n: send(TL.at[n, t], RSL.at[n, d - 1], s_tl.at[n], r_tl.at[n], i, t))

    for a in range(2, LEV + 1):
        n = a - 2
        drain(RSL.at[n], r_tl.at[n])
        total = TL[n, b].astype(F32) + sum7(RSL.at[n])

        @pl.when(odd == 1)
        def _(n=n, total=total):
            UO1[n] = total.astype(BF16)
            send(UO1.at[n], UX.at[n, 1], s_u1.at[n], r_ux.at[n], even_slot, b)
            U[n] = jnp.zeros((64, 128), F32)

        @pl.when(odd == 0)
        def _(n=n, total=total):
            U[n] = total
            UX[n, 0] = jnp.zeros((64, 128), BF16)

    def upward(n):
        @pl.when(lev == 1)
        def _():
            drain(UX.at[n, 1], r_ux.at[n])

        @pl.when(lev != 1)
        def _():
            drain(UX.at[n], r_ux.at[n])

        return U[n] + UX[n, 0].astype(F32) + UX[n, 1].astype(F32)

    @pl.when(owner)
    def _():
        @pl.when(lev == 1)
        def _():
            drain(RX.at[pl.ds(0, 15)], r_rx)

        @pl.when(lev != 1)
        def _():
            drain(RX, r_rx)

        rs = sr_in[0].astype(F32)
        for c in range(2 * NB):
            rs = rs - RX[c].astype(F32)
        SR[b] = rs.astype(BF16)
        others(lambda d, t: send(SR.at[b], SR.at[b], s_sr, r_sr, i, t))
        drain(SR.at[pl.ds(0, 7)], r_sr)
        sy = dot_t(full(SR), si[0])
        SA[...] = sy
        syb = sy.astype(BF16)

        for a in range(2, LEV + 1):
            n = a - 2

            @pl.when(lev == a - 1)
            def _(a=a, n=n):
                spread(TC, dot_t(syb, sc[0, a - 1]))
                others(lambda d, t: send(TC.at[t], RX.at[pb * NB + b], s_tc, r_rx, parent, t))
                TC[b] = (TC[b].astype(F32) + upward(n)).astype(BF16)
                send(TC.at[b], RX.at[pb * NB + b], s_tc, r_rx, parent, b)

            if a > 2:
                @pl.when(lev < a - 1)
                def _(a=a, n=n):
                    spread(TN.at[a - 3], dot_t(syb, sc[0, a - 1]))
                    others(lambda d, t: send(TN.at[a - 3, t], RSS.at[a - 3, d - 1], s_tn.at[a - 3], r_tn.at[a - 3], i, t))

        for a in range(3, LEV + 1):
            n = a - 2

            @pl.when(lev < a - 1)
            def _(a=a, n=n):
                drain(RSS.at[a - 3], r_tn.at[a - 3])
                UO2[n] = (TN[a - 3, b].astype(F32) + sum7(RSS.at[a - 3]) + upward(n)).astype(BF16)
                send(UO2.at[n], UX.at[n, pb], s_u2.at[n], r_ux.at[n], parent, b)

    def leaf_part(a):
        LA[...] = LA[...] - pat[0, a - 1].astype(F32) * jnp.dot(full(XF.at[a - 1]), lc[0, a - 1], preferred_element_type=F32)

    for a in range(LEV, 1, -1):
        @pl.when(lev < a)
        def _(a=a):
            drain(XF.at[a - 1], r_xf.at[a - 1])

            @pl.when(lev >= 2)
            def _():
                all_blk(lambda t: send(XF.at[a - 1, b], XF.at[a - 1, b], s_xf.at[a - 1], r_xf.at[a - 1], kid0, t))
                all_blk(lambda t: send(XF.at[a - 1, b], XF.at[a - 1, b], s_xf.at[a - 1], r_xf.at[a - 1], kid1, t))

            @pl.when((lev == 1) & (a < lev_next))
            def _():
                all_blk(lambda t: send(XF.at[a - 1, b], XF.at[a - 1, b], s_xf.at[a - 1], r_xf.at[a - 1], pair_slot, t))

            SA[...] = SA[...] - jnp.dot(full(XF.at[a - 1]), sc[0, a - 1], preferred_element_type=F32)
            leaf_part(a)

    @pl.when(owner)
    def _():
        spread(PB, jnp.dot(SA[...].astype(BF16), si[0], preferred_element_type=F32))
        others(lambda d, t: send(PB.at[t], RSB.at[d - 1], s_pb, r_pb, i, t))
        drain(RSB, r_pb)
        x = PB[b].astype(F32) + sum7(RSB)
        ssol[0] = x
        own = lev - 1
        XF[own, b] = x.astype(BF16)

        @pl.when(lev >= 2)
        def _():
            all_blk(lambda t: send(XF.at[own, b], XF.at[own, b], s_xo, r_xf.at[own], kid0, t))
            all_blk(lambda t: send(XF.at[own, b], XF.at[own, b], s_xo, r_xf.at[own], kid1, t))

        @pl.when(lev == 1)
        def _():
            all_blk(lambda t: send(XF.at[own, b], XF.at[own, b], s_xo, r_xf.at[own], pair_slot, t))

        others(lambda d, t: send(XF.at[own, b], XF.at[own, b], s_pb, r_xf.at[own], i, t))
        drain(XF.at[own, pl.ds(0, 7)], r_xf.at[own])
        leaf_part(lev)

    @pl.when(lev > LEV)
    def _():
        ssol[0] = jnp.zeros((64, 128), F32)

    for a in range(LEV, 0, -1):
        @pl.when(a < lev)
        def _(a=a):
            drain(XF.at[a - 1], r_xf.at[a - 1])
            leaf_part(a)

    spread(LB, jnp.dot(LA[...].astype(BF16), li[0], preferred_element_type=F32))
    others(lambda d, t: send(LB.at[t], RLB.at[d - 1], s_lb, r_lb, i, t))
    drain(RLB, r_lb)
    lsol[0] = LB[b].astype(F32) + sum7(RLB)

    drain(LR.at[pl.ds(0, 7)], s_lr)

    @pl.when(odd == 1)
    def _():
        drain(T1, s_t1)
        for n in range(LEV - 1):
            drain(UO1.at[n], s_u1.at[n])

    @pl.when(odd == 0)
    def _():
        drain(T1.at[pl.ds(0, 7)], s_t1)

    for n in range(LEV - 1):
        drain(TL.at[n, pl.ds(0, 7)], s_tl.at[n])
    drain(LB.at[pl.ds(0, 7)], s_lb)

    @pl.when(owner)
    def _():
        drain(SR.at[pl.ds(0, 7)], s_sr)
        drain(RX.at[pl.ds(0, 14)], s_pb)

        @pl.when(lev >= 2)
        def _():
            drain(RX, s_xo)

        @pl.when(lev == 1)
        def _():
            drain(PB, s_xo)

        @pl.when(lev < LEV)
        def _():
            drain(TC, s_tc)

    for a in range(3, LEV + 1):
        @pl.when(lev < a - 1)
        def _(a=a):
            drain(TN.at[a - 3, pl.ds(0, 7)], s_tn.at[a - 3])
            drain(UO2.at[a - 2], s_u2.at[a - 2])

    for a in range(LEV, 1, -1):
        @pl.when((lev < a) & (lev >= 2))
        def _(a=a):
            drain(RX, s_xf.at[a - 1])

        @pl.when((lev == 1) & (a < lev_next))
        def _(a=a):
            drain(PB, s_xf.at[a - 1])


def body(*args):
    chunk = (64, 128)
    vmem = pl.BlockSpec(memory_space=pltpu.VMEM)
    dma = pltpu.SemaphoreType.DMA

    def chunks(*lead, dtype=BF16):
        return pltpu.VMEM(lead + chunk, dtype)

    scratch = [
        chunks(8), chunks(dtype=F32), chunks(8), chunks(5, 8), chunks(5, 7), chunks(5, dtype=F32),
        chunks(5), chunks(5), chunks(5, 2), chunks(16), chunks(8), chunks(dtype=F32), chunks(8),
        chunks(4, 8), chunks(4, 7), chunks(6, 8), chunks(8), chunks(7), chunks(8), chunks(7),
        chunks(dtype=F32), chunks(dtype=F32),
        dma, dma, dma, dma((5,)), dma((5,)), dma((5,)), dma((5,)), dma((5,)), dma, dma, dma, dma,
        dma((4,)), dma((4,)), dma((6,)), dma, dma((6,)), dma, dma, dma, dma,
    ]
    out = jax.ShapeDtypeStruct((1,) + chunk, F32)
    return pl.pallas_call(
        kernel,
        out_shape=(out, out),
        in_specs=[vmem] * 6 + [pl.BlockSpec(memory_space=pltpu.SMEM)],
        out_specs=(vmem, vmem),
        scratch_shapes=scratch,
        compiler_params=pltpu.CompilerParams(collective_id=0, has_side_effects=True, vmem_limit_bytes=40 * 2**20),
        name="solve",
    )(*args)


def solution(mesh):
    in_specs = (
        P("leaf", "blk", None),
        P("leaf", None, None, "blk"),
        P("leaf", "blk", None),
        P("leaf", None, None, "blk"),
        P("leaf", None, "blk"),
        P("leaf", None, "blk"),
        P("leaf", None),
    )
    out_specs = (P("leaf", None, "blk"), P("leaf", None, "blk"))
    return jax.shard_map(body, mesh=mesh, in_specs=in_specs, out_specs=out_specs, check_vma=False)
```

time: 1770 us -> 176 us (0.10)
  waiting for transfers between devices: 1450 us -> 0 us
  starting transfers between devices: 223 us -> 0 us
  Pallas kernels: 0 us -> 165 us
  other arithmetic: 30.4 us -> 0 us
  blocking collectives: 29.7 us -> 0 us
    psum x12 -> x0, waiting for transfers between devices: 918 us -> none  [group_total(): return lax.psum(summed, 'blk')]
    ppermute x42 -> x0, waiting for transfers between devices: 493 us -> none  [swapped(): return lax.ppermute(block, axis, route)]
    ppermute x42 -> x0, starting transfers between devices: 223 us -> none  [swapped(): return lax.ppermute(block, axis, route)]
    pallas_call x0 -> x1, Pallas kernels: none -> 165 us  [body(): pl.pallas_call(kernel, out_shape=(out, out), in_specs=[vmem] * 6 + [pl.Bl...]
    unnamed x14 -> x0, waiting for transfers between devices: 36.1 us -> none
    all_gather x2 -> x0, blocking collectives: 29.7 us -> none  [the longest x1 18.4 us: body(): lax.all_gather(leaf_right[0], 'blk', axis=1, tiled=True)]
    add x51 -> x0, other arithmetic: 22.8 us -> none  [the longest x42 10.1 us: group_total(): summed = summed + swapped(summed, 'leaf', bit_pos)]
  transfers between devices with their start and end apart: 55 -> 0, of which waited for: 54 -> 0; matrix products, arithmetic and copies ran while one was open for 0% -> 0% of each run, Pallas kernels for 0% -> 0%
where the time goes in v1:
time: 176 us; the launch traced here: 173 us
  Pallas kernels  165 us (94%)
  local copies, waits for them, and re-layouts  8.03 us (5%)
    pallas_call x1, Pallas kernels, body(): pl.pallas_call(kernel, out_shape=(out, out), in_specs=[vmem] * 6 + [pl.Bl...  165 us
    unnamed x16, local copies, waits for them, and re-layouts  8.03 us

profile of v1, /device:TPU:1, one launch (start us, length us, event | category | flops | bytes accessed | tf_op | source)
XLA Modules:
  0.0 173.3 jit_solution(11552918622167237323)
XLA Ops:
  0.6 0.0 copy-start
  0.6 1.4 copy-done
  2.0 0.0 copy-start.1
  2.0 1.4 copy-done.1
  3.4 0.0 copy-start.2
  3.5 0.9 copy-done.2
  4.4 0.0 copy-start.3
  4.4 0.9 copy-done.3
  5.4 0.0 copy-start.4
  5.4 0.7 copy-done.4
  6.1 0.0 copy-start.5
  6.1 0.7 copy-done.5
  6.8 0.0 copy-start.6
  6.8 0.7 copy-done.6
  7.4 164.6 %solve.1 = (f32[1,64,128]{2,1,0:T(8,128)S(1)}, f32[1,64,128]{2,1,0:T(8,128)S(1)}) custom-call(bf16[1,128,1024]{2,1,0:T(8,128)(2,1)S(1)} %copy-done.2, bf16[1,6,1024,128]{3,2,1,0:T(8,128)(2,1)S(1)} %copy-done, bf16[1,128,1024]{2,1,0:T(8,128)(2,1)S(1)} %copy-done.3, bf16[1,6,1024,128]{3,2,1,0:T(8,128)(2,1)S(1)} %copy-done.1, ...), custom_call_target="tpu_custom_call" | custom-call | tf_op jit(solution)/shard_map/solve/pallas_call | solution.py:322
  172.0 0.6 copy.11
  172.7 0.6 copy.12
Async XLA Ops:
  0.6 1.4 copy-start
  2.0 1.4 copy-start.1
  3.4 0.9 copy-start.2
  4.4 0.9 copy-start.3
  5.4 0.7 copy-start.4
  6.1 0.7 copy-start.5
  6.8 0.7 copy-start.6

commit v2 on v1

--- a/solution.py
+++ b/solution.py
@@ -25,8 +25,8 @@
     return lax.dot_general(a, b, (((1,), (1,)), ((), ())), preferred_element_type=F32)
 
 
-def kernel(li, lc, si, sc, lr_in, sr_in, pat, lsol, ssol,
-           LR, LY, T1, TL, RSL, U, UO1, UO2, UX, RX, SR, SY, TC, TN, RSS, XF, PB, RSB, LB, RLB, SA, LA,
+def kernel(li_in, lc_in, si_in, sc_in, lr_in, sr_in, pat, lsol, ssol,
+           li, lc, si, sc, SRI, ld, LR, LY, T1, TL, RSL, U, UO1, UO2, UX, RX, SR, SY, TC, TN, RSS, XF, PB, RSB, LB, RLB, SA, LA,
            s_lr, r_lr, s_t1, s_tl, r_tl, s_u1, s_u2, r_ux, r_rx, s_sr, r_sr, s_tc, s_tn, r_tn,
            s_xf, s_xo, r_xf, s_pb, r_pb, s_lb, r_lb):
     i = lax.axis_index("leaf")
@@ -74,6 +74,17 @@
             total = total + ref[d].astype(F32)
         return total
 
+    loads = [
+        pltpu.make_async_copy(lr_in.at[0], LR.at[b], ld.at[0]),
+        pltpu.make_async_copy(li_in, li, ld.at[1]),
+        pltpu.make_async_copy(lc_in, lc, ld.at[2]),
+        pltpu.make_async_copy(sr_in, SRI, ld.at[3]),
+        pltpu.make_async_copy(si_in, si, ld.at[4]),
+        pltpu.make_async_copy(sc_in, sc, ld.at[5]),
+    ]
+    for load in loads:
+        load.start()
+
     barrier = pltpu.get_barrier_semaphore()
 
     def greet(leaf, blk):
@@ -99,14 +110,16 @@
              + jnp.where((lev >= 2) & owner, 16, 0))
     pl.semaphore_wait(barrier, peers)
 
-    LR[b] = lr_in[0]
+    loads[0].wait()
     others(lambda d, t: send(LR.at[b], LR.at[b], s_lr, r_lr, i, t))
     drain(LR.at[pl.ds(0, 7)], r_lr)
+    loads[1].wait()
     ly = dot_t(full(LR), li[0])
     LY[...] = ly
     LA[...] = ly
     lyb = ly.astype(BF16)
 
+    loads[2].wait()
     spread(T1, dot_t(lyb, lc[0, 0]) * pat[0, 0].astype(F32))
 
     @pl.when(odd == 1)
@@ -150,6 +163,9 @@
 
         return U[n] + UX[n, 0].astype(F32) + UX[n, 1].astype(F32)
 
+    for load in loads[3:]:
+        load.wait()
+
     @pl.when(owner)
     def _():
         @pl.when(lev == 1)
@@ -160,7 +176,7 @@
         def _():
             drain(RX, r_rx)
 
-        rs = sr_in[0].astype(F32)
+        rs = SRI[0].astype(F32)
         for c in range(2 * NB):
             rs = rs - RX[c].astype(F32)
         SR[b] = rs.astype(BF16)
@@ -311,6 +327,8 @@
         return pltpu.VMEM(lead + chunk, dtype)
 
     scratch = [
+        pltpu.VMEM((1, 128, 1024), BF16), pltpu.VMEM((1, 6, 1024, 128), BF16),
+        pltpu.VMEM((1, 128, 1024), BF16), pltpu.VMEM((1, 6, 1024, 128), BF16), chunks(1), dma((6,)),
         chunks(8), chunks(dtype=F32), chunks(8), chunks(5, 8), chunks(5, 7), chunks(5, dtype=F32),
         chunks(5), chunks(5), chunks(5, 2), chunks(16), chunks(8), chunks(dtype=F32), chunks(8),
         chunks(4, 8), chunks(4, 7), chunks(6, 8), chunks(8), chunks(7), chunks(8), chunks(7),
@@ -322,10 +340,10 @@
     return pl.pallas_call(
         kernel,
         out_shape=(out, out),
-        in_specs=[vmem] * 6 + [pl.BlockSpec(memory_space=pltpu.SMEM)],
+        in_specs=[pl.BlockSpec(memory_space=pl.ANY)] * 6 + [pl.BlockSpec(memory_space=pltpu.SMEM)],
         out_specs=(vmem, vmem),
         scratch_shapes=scratch,
-        compiler_params=pltpu.CompilerParams(collective_id=0, has_side_effects=True, vmem_limit_bytes=40 * 2**20),
+        compiler_params=pltpu.CompilerParams(collective_id=0, has_side_effects=True, vmem_limit_bytes=56 * 2**20),
         name="solve",
     )(*args)
 

time: 176 us -> 171 us (0.972)
  local copies, waits for them, and re-layouts: 8.03 us -> 2.75 us
    unnamed x16 -> x2, local copies, waits for them, and re-layouts: 8.03 us -> 2.75 us
where the time goes in v2:
time: 171 us; the launch traced here: 169 us
  Pallas kernels  165 us (96%)
  local copies, waits for them, and re-layouts  2.75 us (2%)
    pallas_call x1, Pallas kernels, body(): pl.pallas_call(kernel, out_shape=(out, out), in_specs=[pl.BlockSpec(memor...  165 us

profile of v2, /device:TPU:1, one launch (start us, length us, event | category | flops | bytes accessed | tf_op | source)
XLA Modules:
  0.0 168.6 jit_solution(8538716309174129259)
XLA Ops:
  0.6 165.2 %solve.1 = (f32[1,64,128]{2,1,0:T(8,128)}, f32[1,64,128]{2,1,0:T(8,128)}) custom-call(bf16[1,128,1024]{2,1,0:T(8,128)(2,1)} %li_in.1, bf16[1,6,1024,128]{3,2,1,0:T(8,128)(2,1)} %lc_in.1, bf16[1,128,1024]{2,1,0:T(8,128)(2,1)} %si_in.1, bf16[1,6,1024,128]{3,2,1,0:T(8,128)(2,1)} %sc_in.1, bf16[1,64,128]{2,1,0:T(8,128)(2,1)} %lr_in.1, ...), custom_call_target="tpu_custom_call" | custom-call | tf_op jit(solution)/shard_map/solve/pallas_call | solution.py:340
  165.8 1.4 copy.11
  167.2 1.4 copy.12

commit v3 on v1

v3 whole, which is shorter than its diff:
```python
import jax
import jax.numpy as jnp
from jax import lax
from jax.experimental import pallas as pl
from jax.experimental.pallas import tpu as pltpu
from jax.sharding import PartitionSpec as P

MESH = pl.DeviceIdType.MESH
F32 = jnp.float32
BF16 = jnp.bfloat16
NB = 8
LEV = 6


def tree_place(i):
    lev, half, run = 1, 1, 1
    for n in range(3):
        run = run * ((i // 2**n) % 2)
        lev = lev + run
        half = half + run * 2**n
    run = run * ((i // 8) % 2)
    return lev + 3 * run, half


def dot(a, b):
    return jnp.dot(a, b, preferred_element_type=F32)


def dot_t(a, b):
    return lax.dot_general(a, b, (((1,), (1,)), ((), ())), preferred_element_type=F32)


class Names:
    def __init__(self, names, refs):
        for name, ref in zip(names, refs, strict=True):
            setattr(self, name, ref)


def chunks(*lead, dtype=BF16):
    return pltpu.VMEM(lead + (64, 128), dtype)


def sems(*shape):
    return pltpu.SemaphoreType.DMA(shape) if shape else pltpu.SemaphoreType.DMA


def blocks(*shape):
    return pltpu.VMEM(shape, BF16)


SCRATCH = dict(
    li=blocks(1, 128, 1024), lc=blocks(1, 6, 1024, 128), si=blocks(1, 128, 1024), sc=blocks(1, 6, 1024, 128),
    SRI=chunks(1), ld=sems(6),
    LR=chunks(8), LY=chunks(dtype=F32), T1=chunks(8), TL=chunks(5, 8), RSL=chunks(5, 7), U=chunks(5, dtype=F32),
    UO1=chunks(5), UO2=chunks(5), UX=chunks(5, 2),
    s_lr=sems(), r_lr=sems(), s_t1=sems(), s_tl=sems(5), r_tl=sems(5), s_u1=sems(5), s_u2=sems(5), r_ux=sems(5),
    RX=chunks(16), SR=chunks(8), TC=chunks(8), TN=chunks(4, 8), RSS=chunks(4, 7), XF=chunks(6, 8),
    PB=chunks(8), RSB=chunks(7), SA=chunks(dtype=F32), SZ=chunks(dtype=F32), LA=chunks(dtype=F32),
    r_rx=sems(), s_sr=sems(), r_sr=sems(), s_tc=sems(), s_tn=sems(4), r_tn=sems(4),
    s_xf=sems(6), s_xb=sems(2), s_xo=sems(), r_xf=sems(6), s_pb=sems(), r_pb=sems(),
    IG=blocks(8, 128, 128), CG=blocks(2, 8, 1024, 128), VG=blocks(8, 128, 1024), M=blocks(2, 1024, 128), G=blocks(128, 1024),
    s_ig=sems(), r_ig=sems(), l_ig=sems(), s_g=sems(3), ra_g=sems(3), rb_g=sems(3), l_g=sems(3),
    HM=blocks(1024, 128), HG5=blocks(128, 1024), HG6=blocks(128, 1024), H5=chunks(1), H6=chunks(1),
    s_hm=sems(), s_hs=sems(), r_hm=sems(), r_hg5=sems(), r_hg6=sems(), r_h5=sems(), r_h6=sems(),
    RX5=chunks(16), RX6=chunks(16), SR5=chunks(8), SR6=chunks(8), TD=chunks(8), HU=chunks(2), Z5=chunks(dtype=F32),
    r_rx5=sems(), r_rx6=sems(), s_r5=sems(), r_r5=sems(), s_r6=sems(), r_r6=sems(), s_td=sems(), r_hu=sems(),
    HX=chunks(dtype=F32), HY=chunks(dtype=F32), s_hx=sems(), r_hx=sems(),
    LB=chunks(8), RLB=chunks(7), s_lb=sems(), r_lb=sems(),
)


def kernel(li_in, lc_in, si_in, sc_in, lr_in, sr_in, pat, lsol, ssol, *scratch):
    v = Names(SCRATCH, scratch)
    i = lax.axis_index("leaf")
    b = lax.axis_index("blk")
    x, z = i // 16, i % 16
    core = b % 2
    mate = b + 1 - 2 * core
    lev, half = tree_place(i)
    lev_next, _ = tree_place(i + 1)
    odd = i % 2
    even_slot = i - odd
    pair_slot = i + 1 - 2 * odd
    side = (i // (2 * half)) % 2
    parent = i + half - 2 * half * side
    kid0 = i - half // 2
    kid1 = i + half // 2
    normal = lev <= 4
    host = lev == 4
    own5 = (z == 15) & (x % 2 == 0)
    own6 = (z == 15) & (x == 1)
    x_near = x + 1 - 2 * (x % 2)
    x_far = (x + 2) % 4
    near = x_near * 16 + 7
    far = x_far * 16 + 7
    host_a = (x - x % 2) * 16 + 7
    host_b = host_a + 16
    owner5 = (x - x % 2) * 16 + 15

    def send(src, dst, ssem, rsem, leaf, blk):
        pltpu.make_async_remote_copy(src_ref=src, dst_ref=dst, send_sem=ssem, recv_sem=rsem,
                                     device_id=(leaf, blk), device_id_type=MESH).start()

    def drain(ref, sem):
        pltpu.make_async_copy(ref, ref, sem).wait()

    def others(fn):
        def step(d, c):
            fn(d, (b + d) % NB)
            return c
        lax.fori_loop(1, NB, step, 0)

    def all_blk(fn):
        def step(d, c):
            fn((b + d) % NB)
            return c
        lax.fori_loop(0, NB, step, 0)

    def full(ref):
        return jnp.concatenate([ref[c] for c in range(NB)], axis=1)

    def spread(ref, value):
        for c in range(NB):
            ref[c] = value[:, c * 128:(c + 1) * 128].astype(BF16)

    def total(ref, count):
        acc = ref[0].astype(F32)
        for d in range(1, count):
            acc = acc + ref[d].astype(F32)
        return acc

    loads = [
        pltpu.make_async_copy(lr_in.at[0], v.LR.at[b], v.ld.at[0]),
        pltpu.make_async_copy(li_in, v.li, v.ld.at[1]),
        pltpu.make_async_copy(lc_in, v.lc, v.ld.at[2]),
        pltpu.make_async_copy(sr_in, v.SRI, v.ld.at[3]),
        pltpu.make_async_copy(si_in, v.si, v.ld.at[4]),
        pltpu.make_async_copy(sc_in, v.sc, v.ld.at[5]),
    ]
    for load in loads:
        load.start()

    barrier = pltpu.get_barrier_semaphore()

    def greet(leaf, blk):
        pl.semaphore_signal(barrier, inc=1, device_id=(leaf, blk), device_id_type=MESH)

    pair_is_kin = (lev == 2) | ((lev == 1) & (side == 0))
    has_kids = (lev >= 2) & normal
    others(lambda d, t: greet(i, t))

    @pl.when(host | own5)
    def _():
        @pl.when(host)
        def _():
            greet(owner5, b)
            greet(31, b)

        @pl.when(own5)
        def _():
            greet(host_a, b)
            greet(host_b, b)

    @pl.when(own6)
    def _():
        for h in range(4):
            greet(16 * h + 7, b)

    @pl.when(host)
    def _():
        all_blk(lambda t: greet(near, t))
        all_blk(lambda t: greet(far, t))

    @pl.when(~pair_is_kin)
    def _():
        all_blk(lambda t: greet(pair_slot, t))

    @pl.when(lev <= 3)
    def _():
        all_blk(lambda t: greet(parent, t))

    @pl.when(has_kids)
    def _():
        all_blk(lambda t: greet(kid0, t))
        all_blk(lambda t: greet(kid1, t))

    peers = (7 + jnp.where(pair_is_kin, 0, 8) + jnp.where(lev <= 3, 8, 0) + jnp.where(has_kids, 16, 0)
             + jnp.where(host, 18, 0) + jnp.where(own5, 2, 0) + jnp.where(own6, 4, 0))
    pl.semaphore_wait(barrier, peers)

    loads[0].wait()
    others(lambda d, t: send(v.LR.at[b], v.LR.at[b], v.s_lr, v.r_lr, i, t))
    for load in loads[1:]:
        load.wait()

    @pl.when(own5)
    def _():
        send(v.SRI, v.H5, v.s_hs, v.r_h5, host_a, b)
        send(v.SRI, v.H5, v.s_hs, v.r_h5, host_b, b)

    @pl.when(own6)
    def _():
        for h in range(4):
            send(v.SRI, v.H6, v.s_hs, v.r_h6, 16 * h + 7, b)

    drain(v.LR.at[pl.ds(0, 7)], v.r_lr)
    ly = dot_t(full(v.LR), v.li[0])
    v.LA[...] = ly
    lyb = ly.astype(BF16)
    spread(v.T1, dot_t(lyb, v.lc[0, 0]) * pat[0, 0].astype(F32))

    @pl.when(odd == 1)
    def _():
        all_blk(lambda t: send(v.T1.at[t], v.RX.at[NB + b], v.s_t1, v.r_rx, even_slot, t))

    @pl.when(odd == 0)
    def _():
        v.RX[b] = v.T1[b]
        others(lambda d, t: send(v.T1.at[t], v.RX.at[b], v.s_t1, v.r_rx, i, t))

    for a in range(2, LEV + 1):
        n = a - 2
        spread(v.TL.at[n], dot_t(lyb, v.lc[0, a - 1]) * pat[0, a - 1].astype(F32))
        others(lambda d, t, n=n: send(v.TL.at[n, t], v.RSL.at[n, d - 1], v.s_tl.at[n], v.r_tl.at[n], i, t))

    def gather_start(k, src, dst):
        pltpu.make_async_copy(src, dst.at[b], v.l_g.at[k]).start()
        for dy in range(1, 4):
            send(src, dst.at[b], v.s_g.at[k], v.ra_g.at[k], i, (b + 2 * dy) % NB)
        send(src, dst.at[b], v.s_g.at[k], v.rb_g.at[k], i, mate)

    def gather_pass(k, dst):
        drain(dst.at[pl.ds(0, 3)], v.ra_g.at[k])
        for dy in range(1, 4):
            t = (b + 2 * dy) % NB
            send(dst.at[t], dst.at[t], v.s_g.at[k], v.rb_g.at[k], i, mate)

    def gather_end(k, dst):
        drain(dst.at[pl.ds(0, 4)], v.rb_g.at[k])
        drain(dst.at[b], v.l_g.at[k])

    def inverse_columns_start():
        pltpu.make_async_copy(v.si.at[0, :, pl.ds(pl.multiple_of(b * 128, 128), 128)], v.IG.at[b], v.l_ig).start()
        others(lambda d, t: send(v.si.at[0, :, pl.ds(pl.multiple_of(t * 128, 128), 128)], v.IG.at[b],
                                 v.s_ig, v.r_ig, i, t))

    def inverse_columns_end():
        drain(v.IG.at[pl.ds(0, 7)], v.r_ig)
        drain(v.IG.at[b], v.l_ig)

    def form_m(k):
        columns = v.IG[...].reshape(1024, 128)

        def tile(r, c):
            rows = pl.ds(pl.multiple_of(r * 256, 256), 256)
            left = jnp.concatenate([v.CG[k, s, rows, :] for s in range(NB)], axis=1)
            v.M[k, rows, :] = dot(left, columns).astype(BF16)
            return c
        lax.fori_loop(0, 4, tile, 0)

    def form_g():
        columns = v.IG[...].reshape(1024, 128)

        def tile(r, c):
            cols = pl.ds(pl.multiple_of(r * 256, 256), 256)
            right = v.VG[:, :, cols].reshape(1024, 256)
            v.G[:, cols] = lax.dot_general(columns, right, (((0,), (0,)), ((), ())),
                                           preferred_element_type=F32).astype(BF16)
            return c
        lax.fori_loop(0, 4, tile, 0)

    def products_start():
        inverse_columns_start()
        gather_start(0, v.sc.at[0, lev], v.CG.at[0])
        gather_start(1, v.sc.at[0, lev + 1], v.CG.at[1])

    def products_end():
        inverse_columns_end()
        gather_pass(0, v.CG.at[0])
        gather_end(0, v.CG.at[0])
        form_m(0)
        gather_pass(1, v.CG.at[1])
        gather_end(1, v.CG.at[1])
        form_m(1)

    early = (lev == 3) | (lev == 4)

    @pl.when(early)
    def _():
        products_start()

    @pl.when(own5 | own6)
    def _():
        inverse_columns_start()

        @pl.when(own5)
        def _():
            gather_start(0, v.sc.at[0, 5], v.CG.at[0])

        gather_start(2, v.si.at[0], v.VG)

    for a in range(2, LEV + 1):
        n = a - 2
        drain(v.RSL.at[n], v.r_tl.at[n])
        acc = v.TL[n, b].astype(F32) + total(v.RSL.at[n], 7)

        @pl.when(odd == 1)
        def _(n=n, acc=acc):
            v.UO1[n] = acc.astype(BF16)
            send(v.UO1.at[n], v.UX.at[n, 1], v.s_u1.at[n], v.r_ux.at[n], even_slot, b)
            v.U[n] = jnp.zeros((64, 128), F32)

        @pl.when(odd == 0)
        def _(n=n, acc=acc):
            v.U[n] = acc
            v.UX[n, 0] = jnp.zeros((64, 128), BF16)

    @pl.when(early)
    def _():
        products_end()

    @pl.when(own5 | own6)
    def _():
        inverse_columns_end()

        @pl.when(own5)
        def _():
            gather_pass(0, v.CG.at[0])
            gather_end(0, v.CG.at[0])
            form_m(0)
            send(v.M.at[0], v.HM, v.s_hm, v.r_hm, host_a, b)
            send(v.M.at[0], v.HM, v.s_hm, v.r_hm, host_b, b)

        gather_pass(2, v.VG)
        gather_end(2, v.VG)
        form_g()

        @pl.when(own5)
        def _():
            send(v.G, v.HG5, v.s_hm, v.r_hg5, host_a, b)
            send(v.G, v.HG5, v.s_hm, v.r_hg5, host_b, b)

        @pl.when(own6)
        def _():
            for h in range(4):
                send(v.G, v.HG6, v.s_hm, v.r_hg6, 16 * h + 7, b)

    def upward(n):
        @pl.when(lev == 1)
        def _():
            drain(v.UX.at[n, 1], v.r_ux.at[n])

        @pl.when(lev != 1)
        def _():
            drain(v.UX.at[n], v.r_ux.at[n])

        return v.U[n] + v.UX[n, 0].astype(F32) + v.UX[n, 1].astype(F32)

    def to_parent(n):
        others(lambda d, t: send(v.TC.at[t], v.RX.at[side * NB + b], v.s_tc, v.r_rx, parent, t))
        v.TC[b] = (v.TC[b].astype(F32) + upward(n)).astype(BF16)
        send(v.TC.at[b], v.RX.at[side * NB + b], v.s_tc, v.r_rx, parent, b)

    def over_blk(a, value):
        spread(v.TN.at[a - 3], value)
        others(lambda d, t: send(v.TN.at[a - 3, t], v.RSS.at[a - 3, d - 1], v.s_tn.at[a - 3], v.r_tn.at[a - 3], i, t))

    def far_part_start():
        spread(v.PB, dot(v.SA[...].astype(BF16), v.si[0]))
        others(lambda d, t: send(v.PB.at[t], v.RSB.at[d - 1], v.s_pb, v.r_pb, i, t))

    @pl.when(normal)
    def _():
        @pl.when(lev == 1)
        def _():
            drain(v.RX.at[pl.ds(0, 15)], v.r_rx)

        @pl.when(lev != 1)
        def _():
            drain(v.RX, v.r_rx)

        rs = v.SRI[0].astype(F32) - total(v.RX, 16)
        rsb = rs.astype(BF16)
        v.SR[b] = rsb

        @pl.when(early)
        def _():
            spread(v.TC, dot_t(rsb, v.M[0]))

            @pl.when(lev == 3)
            def _():
                to_parent(2)
                over_blk(5, dot_t(rsb, v.M[1]))

            @pl.when(lev == 4)
            def _():
                v.TC[b] = (v.TC[b].astype(F32) + upward(3)).astype(BF16)
                mine = (x % 2) * NB + b
                v.RX5[mine] = v.TC[b]
                all_blk(lambda t: send(v.TC.at[t], v.RX5.at[mine], v.s_tc, v.r_rx5, near, t))
                others(lambda d, t: send(v.TC.at[t], v.RX5.at[mine], v.s_tc, v.r_rx5, i, t))
                over_blk(6, dot_t(rsb, v.M[1]))

        others(lambda d, t: send(v.SR.at[b], v.SR.at[b], v.s_sr, v.r_sr, i, t))
        drain(v.SR.at[pl.ds(0, 7)], v.r_sr)
        sy = dot_t(full(v.SR), v.si[0])
        v.SA[...] = sy
        syb = sy.astype(BF16)

        for a in (2, 3):
            @pl.when(lev == a - 1)
            def _(a=a):
                spread(v.TC, dot_t(syb, v.sc[0, a - 1]))
                to_parent(a - 2)

        for a in range(3, LEV + 1):
            @pl.when((lev < a - 1) & ((lev <= 2) | ((lev == 3) & (a == 6))))
            def _(a=a):
                over_blk(a, dot_t(syb, v.sc[0, a - 1]))

        for a in range(3, LEV + 1):
            n = a - 2

            @pl.when(lev < a - 1)
            def _(a=a, n=n):
                drain(v.RSS.at[a - 3], v.r_tn.at[a - 3])
                acc = v.TN[a - 3, b].astype(F32) + total(v.RSS.at[a - 3], 7) + upward(n)
                v.UO2[n] = acc.astype(BF16)

                @pl.when(lev <= 3)
                def _():
                    send(v.UO2.at[n], v.UX.at[n, side], v.s_u2.at[n], v.r_ux.at[n], parent, b)

                if a == 6:
                    @pl.when(lev == 4)
                    def _():
                        v.HU[x % 2] = v.UO2[n]
                        send(v.UO2.at[n], v.HU.at[x % 2], v.s_u2.at[n], v.r_hu, near, b)

        @pl.when(lev == 4)
        def _():
            far_part_start()

        @pl.when(lev <= 2)
        def _():
            products_start()
            products_end()

    def leaf_part(a):
        v.LA[...] = v.LA[...] - pat[0, a - 1].astype(F32) * dot(full(v.XF.at[a - 1]), v.lc[0, a - 1])

    def to_kids(n, sem):
        all_blk(lambda t: send(v.XF.at[n, b], v.XF.at[n, b], sem, v.r_xf.at[n], kid0, t))
        all_blk(lambda t: send(v.XF.at[n, b], v.XF.at[n, b], sem, v.r_xf.at[n], kid1, t))

    def to_pair(n, sem):
        all_blk(lambda t: send(v.XF.at[n, b], v.XF.at[n, b], sem, v.r_xf.at[n], pair_slot, t))

    def to_blk(n, sem):
        others(lambda d, t: send(v.XF.at[n, b], v.XF.at[n, b], sem, v.r_xf.at[n], i, t))

    def finish():
        drain(v.RSB, v.r_pb)
        sol = v.PB[b].astype(F32) + total(v.RSB, 7) - v.SZ[...]
        own = lev - 1
        v.XF[own, b] = sol.astype(BF16)

        @pl.when(lev >= 2)
        def _():
            to_kids(own, v.s_xo)

        @pl.when(lev == 1)
        def _():
            to_pair(own, v.s_xo)

        to_blk(own, v.s_pb)
        ssol[0] = sol

    @pl.when(host)
    def _():
        drain(v.RX5.at[pl.ds(0, 15)], v.r_rx5)
        drain(v.H5, v.r_h5)
        rs = (v.H5[0].astype(F32) - total(v.RX5, 16)).astype(BF16)
        v.SR5[b] = rs
        drain(v.HM, v.r_hm)
        spread(v.TD, dot_t(rs, v.HM[...]))
        drain(v.HU.at[0], v.r_hu)
        v.TD[b] = (v.TD[b].astype(F32) + v.HU[0].astype(F32) + v.HU[1].astype(F32)).astype(BF16)
        mine = (x // 2) * NB + b
        v.RX6[mine] = v.TD[b]
        all_blk(lambda t: send(v.TD.at[t], v.RX6.at[mine], v.s_td, v.r_rx6, far, t))
        others(lambda d, t: send(v.TD.at[t], v.RX6.at[mine], v.s_td, v.r_rx6, i, t))
        others(lambda d, t: send(v.SR5.at[b], v.SR5.at[b], v.s_r5, v.r_r5, i, t))
        drain(v.SR5.at[pl.ds(0, 7)], v.r_r5)
        drain(v.HG5, v.r_hg5)
        v.Z5[...] = dot_t(full(v.SR5), v.HG5[...])

        drain(v.RX6.at[pl.ds(0, 15)], v.r_rx6)
        drain(v.H6, v.r_h6)
        v.SR6[b] = (v.H6[0].astype(F32) - total(v.RX6, 16)).astype(BF16)
        others(lambda d, t: send(v.SR6.at[b], v.SR6.at[b], v.s_r6, v.r_r6, i, t))
        drain(v.HG6, v.r_hg6)
        drain(v.SR6.at[pl.ds(0, 7)], v.r_r6)
        sol6 = dot_t(full(v.SR6), v.HG6[...])
        v.XF[5, b] = sol6.astype(BF16)
        to_blk(5, v.s_xb.at[1])
        to_kids(5, v.s_xf.at[5])
        drain(v.XF.at[5, pl.ds(0, 7)], v.r_xf.at[5])
        x6 = full(v.XF.at[5])
        sol5 = v.Z5[...] - dot(x6, v.HM[...])
        v.XF[4, b] = sol5.astype(BF16)
        to_blk(4, v.s_xb.at[0])
        to_kids(4, v.s_xf.at[4])
        part = dot(x6, v.M[1])

        @pl.when(x == 1)
        def _():
            v.HX[...] = sol6
            send(v.HX, v.HY, v.s_hx, v.r_hx, 31, b)

        @pl.when(x % 2 == 0)
        def _():
            v.HX[...] = sol5
            send(v.HX, v.HY, v.s_hx, v.r_hx, owner5, b)

        leaf_part(6)
        drain(v.XF.at[4, pl.ds(0, 7)], v.r_xf.at[4])
        v.SZ[...] = part + dot(full(v.XF.at[4]), v.M[0])
        finish()
        leaf_part(5)

    for a in range(LEV, 1, -1):
        @pl.when((lev <= 3) & (lev < a))
        def _(a=a):
            n = a - 1
            drain(v.XF.at[n], v.r_xf.at[n])

            @pl.when(lev >= 2)
            def _():
                to_kids(n, v.s_xf.at[n])

            @pl.when((lev == 1) & (a < lev_next))
            def _():
                to_pair(n, v.s_xf.at[n])

            @pl.when(a >= lev + 3)
            def _():
                v.SA[...] = v.SA[...] - dot(full(v.XF.at[n]), v.sc[0, n])

            @pl.when(a == lev + 3)
            def _():
                far_part_start()

            @pl.when(a == lev + 2)
            def _():
                v.SZ[...] = dot(full(v.XF.at[n]), v.M[1])

            @pl.when(a == lev + 1)
            def _():
                v.SZ[...] = v.SZ[...] + dot(full(v.XF.at[n]), v.M[0])
                finish()

            leaf_part(a)

    @pl.when(normal)
    def _():
        drain(v.XF.at[lev - 1, pl.ds(0, 7)], v.r_xf.at[lev - 1])
        leaf_part(lev)

    @pl.when(own5 | own6)
    def _():
        drain(v.HY, v.r_hx)
        ssol[0] = v.HY[...]

    @pl.when((z == 15) & (x == 3))
    def _():
        ssol[0] = jnp.zeros((64, 128), F32)

    for a in range(LEV, 0, -1):
        @pl.when(a < lev)
        def _(a=a):
            drain(v.XF.at[a - 1], v.r_xf.at[a - 1])
            leaf_part(a)

    spread(v.LB, dot(v.LA[...].astype(BF16), v.li[0]))
    others(lambda d, t: send(v.LB.at[t], v.RLB.at[d - 1], v.s_lb, v.r_lb, i, t))
    drain(v.RLB, v.r_lb)
    lsol[0] = v.LB[b].astype(F32) + total(v.RLB, 7)

    seven = pl.ds(0, 7)
    drain(v.LR.at[seven], v.s_lr)

    @pl.when(odd == 1)
    def _():
        drain(v.T1, v.s_t1)
        for n in range(LEV - 1):
            drain(v.UO1.at[n], v.s_u1.at[n])

    @pl.when(odd == 0)
    def _():
        drain(v.T1.at[seven], v.s_t1)

    for n in range(LEV - 1):
        drain(v.TL.at[n, seven], v.s_tl.at[n])
    drain(v.LB.at[seven], v.s_lb)

    @pl.when(normal)
    def _():
        drain(v.SR.at[seven], v.s_sr)
        drain(v.RX.at[pl.ds(0, 14)], v.s_pb)
        drain(v.IG.at[seven], v.s_ig)
        drain(v.CG.at[0, seven], v.s_g.at[0])
        drain(v.CG.at[1, seven], v.s_g.at[1])

        @pl.when(lev >= 2)
        def _():
            drain(v.RX, v.s_xo)

        @pl.when(lev == 1)
        def _():
            drain(v.PB, v.s_xo)

        @pl.when(lev <= 3)
        def _():
            drain(v.TC, v.s_tc)

        for a in range(3, LEV + 1):
            @pl.when(lev < a - 1)
            def _(a=a):
                drain(v.TN.at[a - 3, seven], v.s_tn.at[a - 3])
                drain(v.UO2.at[a - 2], v.s_u2.at[a - 2])

    @pl.when(host)
    def _():
        drain(v.RX.at[pl.ds(0, 15)], v.s_tc)
        drain(v.RX.at[pl.ds(0, 15)], v.s_td)
        drain(v.SR5.at[seven], v.s_r5)
        drain(v.SR6.at[seven], v.s_r6)
        for n in range(2):
            drain(v.RX, v.s_xf.at[4 + n])
            drain(v.SR5.at[seven], v.s_xb.at[n])

        @pl.when(x < 3)
        def _():
            drain(v.HX, v.s_hx)

    @pl.when(own5 | own6)
    def _():
        drain(v.IG.at[seven], v.s_ig)
        drain(v.VG.at[seven], v.s_g.at[2])
        drain(v.CG.at[0, pl.ds(0, 4)], v.s_hm)

    @pl.when(own5)
    def _():
        drain(v.CG.at[0, seven], v.s_g.at[0])
        drain(v.PB.at[pl.ds(0, 2)], v.s_hs)

    @pl.when(own6)
    def _():
        drain(v.PB.at[pl.ds(0, 4)], v.s_hs)

    for a in range(LEV, 1, -1):
        @pl.when((lev < a) & ((lev == 2) | (lev == 3)))
        def _(a=a):
            drain(v.RX, v.s_xf.at[a - 1])

        @pl.when((lev == 1) & (a < lev_next))
        def _(a=a):
            drain(v.PB, v.s_xf.at[a - 1])


def body(*args):
    vmem = pl.BlockSpec(memory_space=pltpu.VMEM)
    out = jax.ShapeDtypeStruct((1, 64, 128), F32)
    return pl.pallas_call(
        kernel,
        out_shape=(out, out),
        in_specs=[pl.BlockSpec(memory_space=pl.ANY)] * 6 + [pl.BlockSpec(memory_space=pltpu.SMEM)],
        out_specs=(vmem, vmem),
        scratch_shapes=list(SCRATCH.values()),
        compiler_params=pltpu.CompilerParams(collective_id=0, has_side_effects=True, vmem_limit_bytes=56 * 2**20),
        name="solve",
    )(*args)


def solution(mesh):
    in_specs = (
        P("leaf", "blk", None),
        P("leaf", None, None, "blk"),
        P("leaf", "blk", None),
        P("leaf", None, None, "blk"),
        P("leaf", None, "blk"),
        P("leaf", None, "blk"),
        P("leaf", None),
    )
    out_specs = (P("leaf", None, "blk"), P("leaf", None, "blk"))
    return jax.shard_map(body, mesh=mesh, in_specs=in_specs, out_specs=out_specs, check_vma=False)
```

time: 176 us -> 155 us (0.88); the launches traced: 173 us -> 155 us
  Pallas kernels: 165 us -> 151 us
  local copies, waits for them, and re-layouts: 8.03 us -> 2.75 us
    pallas_call x1, Pallas kernels: 165 us -> 151 us  [body(): pl.pallas_call(kernel, out_shape=(out, out), in_specs=[pl.BlockSpec(memor...]
    unnamed x16 -> x2, local copies, waits for them, and re-layouts: 8.03 us -> 2.75 us
where the time goes in v3:
time: 155 us
  Pallas kernels  151 us (97%)
  local copies, waits for them, and re-layouts  2.75 us (2%)
    pallas_call x1, Pallas kernels, body(): pl.pallas_call(kernel, out_shape=(out, out), in_specs=[pl.BlockSpec(memor...  151 us

profile of v3, /device:TPU:1, one launch (start us, length us, event | category | flops | bytes accessed | tf_op | source)
XLA Modules:
  0.0 154.6 jit_solution(17495657551619609529)
XLA Ops:
  0.6 151.2 %solve.1 = (f32[1,64,128]{2,1,0:T(8,128)}, f32[1,64,128]{2,1,0:T(8,128)}) custom-call(bf16[1,128,1024]{2,1,0:T(8,128)(2,1)} %li_in.1, bf16[1,6,1024,128]{3,2,1,0:T(8,128)(2,1)} %lc_in.1, bf16[1,128,1024]{2,1,0:T(8,128)(2,1)} %si_in.1, bf16[1,6,1024,128]{3,2,1,0:T(8,128)(2,1)} %sc_in.1, bf16[1,64,128]{2,1,0:T(8,128)(2,1)} %lr_in.1, ...), custom_call_target="tpu_custom_call" | custom-call | tf_op jit(solution)/shard_map/solve/pallas_call | solution.py:675
  151.9 1.4 copy.11
  153.2 1.4 copy.12

commit v4 on v3

--- a/solution.py
+++ b/solution.py
@@ -59,9 +59,10 @@
     r_rx=sems(), s_sr=sems(), r_sr=sems(), s_tc=sems(), s_tn=sems(4), r_tn=sems(4),
     s_xf=sems(6), s_xb=sems(2), s_xo=sems(), r_xf=sems(6), s_pb=sems(), r_pb=sems(),
     IG=blocks(8, 128, 128), CG=blocks(2, 8, 1024, 128), VG=blocks(8, 128, 1024), M=blocks(2, 1024, 128), G=blocks(128, 1024),
-    s_ig=sems(), r_ig=sems(), l_ig=sems(), s_g=sems(3), ra_g=sems(3), rb_g=sems(3), l_g=sems(3),
+    CL=blocks(8, 1024, 128), IL=blocks(8, 128, 128), ML=blocks(1024, 128),
+    s_ig=sems(2), r_ig=sems(2), l_ig=sems(2), s_g=sems(4), ru_g=sems(4), rd_g=sems(4), rf_g=sems(4), rm_g=sems(4), l_g=sems(4),
     HM=blocks(1024, 128), HG5=blocks(128, 1024), HG6=blocks(128, 1024), H5=chunks(1), H6=chunks(1),
-    s_hm=sems(), s_hs=sems(), r_hm=sems(), r_hg5=sems(), r_hg6=sems(), r_h5=sems(), r_h6=sems(),
+    s_hm=sems(), s_hr=sems(), s_hs=sems(), r_hm=sems(), r_hg5=sems(), r_hg6=sems(), r_h5=sems(), r_h6=sems(),
     RX5=chunks(16), RX6=chunks(16), SR5=chunks(8), SR6=chunks(8), TD=chunks(8), HU=chunks(2), Z5=chunks(dtype=F32),
     r_rx5=sems(), r_rx6=sems(), s_r5=sems(), r_r5=sems(), s_r6=sems(), r_r6=sems(), s_td=sems(), r_hu=sems(),
     HX=chunks(dtype=F32), HY=chunks(dtype=F32), s_hx=sems(), r_hx=sems(),
@@ -85,6 +86,7 @@
     parent = i + half - 2 * half * side
     kid0 = i - half // 2
     kid1 = i + half // 2
+    gap = half // 4
     normal = lev <= 4
     host = lev == 4
     own5 = (z == 15) & (x % 2 == 0)
@@ -145,116 +147,108 @@
     def greet(leaf, blk):
         pl.semaphore_signal(barrier, inc=1, device_id=(leaf, blk), device_id_type=MESH)
 
-    pair_is_kin = (lev == 2) | ((lev == 1) & (side == 0))
+    pair_is_kin = (lev == 2) | (lev == 3) | ((lev == 1) & ((side == 0) | (i % 8 == 2)))
     has_kids = (lev >= 2) & normal
+    has_grandkids = (lev == 3) | (lev == 4)
     others(lambda d, t: greet(i, t))
 
-    @pl.when(host | own5)
-    def _():
-        @pl.when(host)
-        def _():
-            greet(owner5, b)
-            greet(31, b)
-
-        @pl.when(own5)
-        def _():
-            greet(host_a, b)
-            greet(host_b, b)
+    @pl.when(host)
+    def _():
+        greet(owner5, b)
+        greet(31, b)
+        greet(near, b)
+        greet(far, b)
+
+    @pl.when(own5)
+    def _():
+        greet(host_a, b)
+        greet(host_b, b)
 
     @pl.when(own6)
     def _():
         for h in range(4):
             greet(16 * h + 7, b)
 
-    @pl.when(host)
-    def _():
-        all_blk(lambda t: greet(near, t))
-        all_blk(lambda t: greet(far, t))
-
     @pl.when(~pair_is_kin)
     def _():
-        all_blk(lambda t: greet(pair_slot, t))
+        greet(pair_slot, b)
 
     @pl.when(lev <= 3)
     def _():
-        all_blk(lambda t: greet(parent, t))
+        greet(parent, b)
+
+    @pl.when(lev == 1)
+    def _():
+        greet(i - i % 8 + 3, b)
+
+    @pl.when(lev == 2)
+    def _():
+        greet(i - z + 7, b)
+
+    @pl.when(z == 13)
+    def _():
+        greet(i + 2, b)
+
+    @pl.when(z == 15)
+    def _():
+        greet(i - 2, b)
 
     @pl.when(has_kids)
     def _():
-        all_blk(lambda t: greet(kid0, t))
-        all_blk(lambda t: greet(kid1, t))
-
-    peers = (7 + jnp.where(pair_is_kin, 0, 8) + jnp.where(lev <= 3, 8, 0) + jnp.where(has_kids, 16, 0)
-             + jnp.where(host, 18, 0) + jnp.where(own5, 2, 0) + jnp.where(own6, 4, 0))
+        greet(kid0, b)
+        greet(kid1, b)
+
+    @pl.when(has_grandkids)
+    def _():
+        for kid in (kid0, kid1):
+            greet(kid - gap, b)
+            greet(kid + gap, b)
+
+    peers = (7 + jnp.where(pair_is_kin, 0, 1) + jnp.where(lev <= 3, 1, 0) + jnp.where(lev <= 2, 1, 0)
+             + jnp.where((z == 13) | (z == 15), 1, 0)
+             + jnp.where(has_kids, 2, 0) + jnp.where(has_grandkids, 4, 0)
+             + jnp.where(host, 4, 0) + jnp.where(own5, 2, 0) + jnp.where(own6, 4, 0))
     pl.semaphore_wait(barrier, peers)
 
-    loads[0].wait()
-    others(lambda d, t: send(v.LR.at[b], v.LR.at[b], v.s_lr, v.r_lr, i, t))
-    for load in loads[1:]:
-        load.wait()
-
-    @pl.when(own5)
-    def _():
-        send(v.SRI, v.H5, v.s_hs, v.r_h5, host_a, b)
-        send(v.SRI, v.H5, v.s_hs, v.r_h5, host_b, b)
-
-    @pl.when(own6)
-    def _():
-        for h in range(4):
-            send(v.SRI, v.H6, v.s_hs, v.r_h6, 16 * h + 7, b)
-
-    drain(v.LR.at[pl.ds(0, 7)], v.r_lr)
-    ly = dot_t(full(v.LR), v.li[0])
-    v.LA[...] = ly
-    lyb = ly.astype(BF16)
-    spread(v.T1, dot_t(lyb, v.lc[0, 0]) * pat[0, 0].astype(F32))
-
-    @pl.when(odd == 1)
-    def _():
-        all_blk(lambda t: send(v.T1.at[t], v.RX.at[NB + b], v.s_t1, v.r_rx, even_slot, t))
-
-    @pl.when(odd == 0)
-    def _():
-        v.RX[b] = v.T1[b]
-        others(lambda d, t: send(v.T1.at[t], v.RX.at[b], v.s_t1, v.r_rx, i, t))
-
-    for a in range(2, LEV + 1):
-        n = a - 2
-        spread(v.TL.at[n], dot_t(lyb, v.lc[0, a - 1]) * pat[0, a - 1].astype(F32))
-        others(lambda d, t, n=n: send(v.TL.at[n, t], v.RSL.at[n, d - 1], v.s_tl.at[n], v.r_tl.at[n], i, t))
+    up, down = (b + 2) % NB, (b + 6) % NB
+    relay_from, relay_to = (b + 6 + 4 * core) % NB, (b + 2 + 4 * core) % NB
 
     def gather_start(k, src, dst):
         pltpu.make_async_copy(src, dst.at[b], v.l_g.at[k]).start()
-        for dy in range(1, 4):
-            send(src, dst.at[b], v.s_g.at[k], v.ra_g.at[k], i, (b + 2 * dy) % NB)
-        send(src, dst.at[b], v.s_g.at[k], v.rb_g.at[k], i, mate)
-
-    def gather_pass(k, dst):
-        drain(dst.at[pl.ds(0, 3)], v.ra_g.at[k])
-        for dy in range(1, 4):
-            t = (b + 2 * dy) % NB
-            send(dst.at[t], dst.at[t], v.s_g.at[k], v.rb_g.at[k], i, mate)
+        send(src, dst.at[b], v.s_g.at[k], v.ru_g.at[k], i, up)
+        send(src, dst.at[b], v.s_g.at[k], v.rd_g.at[k], i, down)
+        send(src, dst.at[b], v.s_g.at[k], v.rm_g.at[k], i, mate)
+
+    def gather_relay(k, dst):
+        drain(dst.at[down], v.ru_g.at[k])
+        drain(dst.at[up], v.rd_g.at[k])
+        send(dst.at[relay_from], dst.at[relay_from], v.s_g.at[k], v.rf_g.at[k], i, relay_to)
+        send(dst.at[down], dst.at[down], v.s_g.at[k], v.rm_g.at[k], i, mate)
+        send(dst.at[up], dst.at[up], v.s_g.at[k], v.rm_g.at[k], i, mate)
 
     def gather_end(k, dst):
-        drain(dst.at[pl.ds(0, 4)], v.rb_g.at[k])
+        opposite = (b + 4) % NB
+        drain(dst.at[opposite], v.rf_g.at[k])
+        send(dst.at[opposite], dst.at[opposite], v.s_g.at[k], v.rm_g.at[k], i, mate)
+        drain(dst.at[pl.ds(0, 4)], v.rm_g.at[k])
         drain(dst.at[b], v.l_g.at[k])
 
-    def inverse_columns_start():
-        pltpu.make_async_copy(v.si.at[0, :, pl.ds(pl.multiple_of(b * 128, 128), 128)], v.IG.at[b], v.l_ig).start()
-        others(lambda d, t: send(v.si.at[0, :, pl.ds(pl.multiple_of(t * 128, 128), 128)], v.IG.at[b],
-                                 v.s_ig, v.r_ig, i, t))
-
-    def inverse_columns_end():
-        drain(v.IG.at[pl.ds(0, 7)], v.r_ig)
-        drain(v.IG.at[b], v.l_ig)
-
-    def form_m(k):
-        columns = v.IG[...].reshape(1024, 128)
+    def columns_start(k, src, dst):
+        pltpu.make_async_copy(src.at[0, :, pl.ds(pl.multiple_of(b * 128, 128), 128)], dst.at[b], v.l_ig.at[k]).start()
+        others(lambda d, t: send(src.at[0, :, pl.ds(pl.multiple_of(t * 128, 128), 128)], dst.at[b],
+                                 v.s_ig.at[k], v.r_ig.at[k], i, t))
+
+    def columns_end(k, dst):
+        drain(dst.at[pl.ds(0, 7)], v.r_ig.at[k])
+        drain(dst.at[b], v.l_ig.at[k])
+
+    def form_m(out, gathered, inverse):
+        columns = inverse[...].reshape(1024, 128)
 
         def tile(r, c):
             rows = pl.ds(pl.multiple_of(r * 256, 256), 256)
-            left = jnp.concatenate([v.CG[k, s, rows, :] for s in range(NB)], axis=1)
-            v.M[k, rows, :] = dot(left, columns).astype(BF16)
+            left = jnp.concatenate([gathered[s, rows, :] for s in range(NB)], axis=1)
+            out[rows, :] = dot(left, columns).astype(BF16)
             return c
         lax.fori_loop(0, 4, tile, 0)
 
@@ -269,35 +263,82 @@
             return c
         lax.fori_loop(0, 4, tile, 0)
 
-    def products_start():
-        inverse_columns_start()
+    early = (lev == 3) | (lev == 4)
+
+    def products_start0():
+        columns_start(0, v.si, v.IG)
         gather_start(0, v.sc.at[0, lev], v.CG.at[0])
+
+    def products_start1():
+        gather_relay(0, v.CG.at[0])
         gather_start(1, v.sc.at[0, lev + 1], v.CG.at[1])
 
     def products_end():
-        inverse_columns_end()
-        gather_pass(0, v.CG.at[0])
+        columns_end(0, v.IG)
         gather_end(0, v.CG.at[0])
-        form_m(0)
-        gather_pass(1, v.CG.at[1])
+        gather_relay(1, v.CG.at[1])
+        form_m(v.M.at[0], v.CG.at[0], v.IG)
         gather_end(1, v.CG.at[1])
-        form_m(1)
-
-    early = (lev == 3) | (lev == 4)
+        form_m(v.M.at[1], v.CG.at[1], v.IG)
+
+    def leaf_product():
+        columns_start(1, v.li, v.IL)
+        gather_start(3, v.lc.at[0, 0], v.CL)
+        gather_relay(3, v.CL)
+        columns_end(1, v.IL)
+        gather_end(3, v.CL)
+        form_m(v.ML, v.CL, v.IL)
+
+    loads[0].wait()
+    others(lambda d, t: send(v.LR.at[b], v.LR.at[b], v.s_lr, v.r_lr, i, t))
+    for load in loads[1:]:
+        load.wait()
+
+    @pl.when(own5)
+    def _():
+        send(v.SRI, v.H5, v.s_hs, v.r_h5, host_a, b)
+        send(v.SRI, v.H5, v.s_hs, v.r_h5, host_b, b)
+
+    @pl.when(own6)
+    def _():
+        for h in range(4):
+            send(v.SRI, v.H6, v.s_hs, v.r_h6, 16 * h + 7, b)
+
+    drain(v.LR.at[pl.ds(0, 7)], v.r_lr)
+    ly = dot_t(full(v.LR), v.li[0])
+    v.LA[...] = ly
+    lyb = ly.astype(BF16)
+    spread(v.T1, dot_t(lyb, v.lc[0, 0]) * pat[0, 0].astype(F32))
+
+    @pl.when(odd == 1)
+    def _():
+        all_blk(lambda t: send(v.T1.at[t], v.RX.at[NB + b], v.s_t1, v.r_rx, even_slot, t))
+
+    @pl.when(odd == 0)
+    def _():
+        v.RX[b] = v.T1[b]
+        others(lambda d, t: send(v.T1.at[t], v.RX.at[b], v.s_t1, v.r_rx, i, t))
+
+    for a in range(2, LEV + 1):
+        n = a - 2
+        spread(v.TL.at[n], dot_t(lyb, v.lc[0, a - 1]) * pat[0, a - 1].astype(F32))
+        others(lambda d, t, n=n: send(v.TL.at[n, t], v.RSL.at[n, d - 1], v.s_tl.at[n], v.r_tl.at[n], i, t))
 
     @pl.when(early)
     def _():
-        products_start()
+        products_start0()
 
     @pl.when(own5 | own6)
     def _():
-        inverse_columns_start()
+        columns_start(0, v.si, v.IG)
 
         @pl.when(own5)
         def _():
             gather_start(0, v.sc.at[0, 5], v.CG.at[0])
 
-        gather_start(2, v.si.at[0], v.VG)
+        @pl.when(own6)
+        def _():
+            gather_start(2, v.si.at[0], v.VG)
 
     for a in range(2, LEV + 1):
         n = a - 2
@@ -317,33 +358,54 @@
 
     @pl.when(early)
     def _():
+        products_start1()
         products_end()
 
+        @pl.when(host & (x % 2 == 0))
+        def _():
+            drain(v.HM, v.r_hm)
+            send(v.HM, v.HM, v.s_hr, v.r_hm, near, b)
+
+        @pl.when(host & (x == 1))
+        def _():
+            drain(v.HG6, v.r_hg6)
+            for h in (0, 2, 3):
+                send(v.HG6, v.HG6, v.s_hr, v.r_hg6, 16 * h + 7, b)
+
     @pl.when(own5 | own6)
     def _():
-        inverse_columns_end()
-
         @pl.when(own5)
         def _():
-            gather_pass(0, v.CG.at[0])
+            gather_relay(0, v.CG.at[0])
+            gather_start(2, v.si.at[0], v.VG)
+
+        @pl.when(own6)
+        def _():
+            gather_relay(2, v.VG)
+
+        columns_end(0, v.IG)
+
+        @pl.when(own5)
+        def _():
             gather_end(0, v.CG.at[0])
-            form_m(0)
+            form_m(v.M.at[0], v.CG.at[0], v.IG)
             send(v.M.at[0], v.HM, v.s_hm, v.r_hm, host_a, b)
-            send(v.M.at[0], v.HM, v.s_hm, v.r_hm, host_b, b)
-
-        gather_pass(2, v.VG)
+            gather_relay(2, v.VG)
+
         gather_end(2, v.VG)
         form_g()
 
         @pl.when(own5)
         def _():
             send(v.G, v.HG5, v.s_hm, v.r_hg5, host_a, b)
-            send(v.G, v.HG5, v.s_hm, v.r_hg5, host_b, b)
 
         @pl.when(own6)
         def _():
-            for h in range(4):
-                send(v.G, v.HG6, v.s_hm, v.r_hg6, 16 * h + 7, b)
+            send(v.G, v.HG6, v.s_hm, v.r_hg6, 23, b)
+
+    @pl.when(z == 15)
+    def _():
+        leaf_product()
 
     def upward(n):
         @pl.when(lev == 1)
@@ -443,18 +505,22 @@
 
         @pl.when(lev <= 2)
         def _():
-            products_start()
+            products_start0()
+            products_start1()
             products_end()
+
+        @pl.when(lev <= 3)
+        def _():
+            leaf_product()
 
     def leaf_part(a):
         v.LA[...] = v.LA[...] - pat[0, a - 1].astype(F32) * dot(full(v.XF.at[a - 1]), v.lc[0, a - 1])
 
-    def to_kids(n, sem):
-        all_blk(lambda t: send(v.XF.at[n, b], v.XF.at[n, b], sem, v.r_xf.at[n], kid0, t))
-        all_blk(lambda t: send(v.XF.at[n, b], v.XF.at[n, b], sem, v.r_xf.at[n], kid1, t))
-
-    def to_pair(n, sem):
-        all_blk(lambda t: send(v.XF.at[n, b], v.XF.at[n, b], sem, v.r_xf.at[n], pair_slot, t))
+    def to_slots(n, sem, *slots):
+        def each(t):
+            for slot in slots:
+                send(v.XF.at[n, b], v.XF.at[n, b], sem, v.r_xf.at[n], slot, t)
+        all_blk(each)
 
     def to_blk(n, sem):
         others(lambda d, t: send(v.XF.at[n, b], v.XF.at[n, b], sem, v.r_xf.at[n], i, t))
@@ -467,13 +533,23 @@
 
         @pl.when(lev >= 2)
         def _():
-            to_kids(own, v.s_xo)
+            to_slots(own, v.s_xo, kid0, kid1)
 
         @pl.when(lev == 1)
         def _():
-            to_pair(own, v.s_xo)
+            to_slots(own, v.s_xo, pair_slot)
 
         to_blk(own, v.s_pb)
+
+        @pl.when(lev >= 3)
+        def _():
+            to_slots(own, v.s_xo, kid0 + gap, kid1 - gap)
+            to_slots(own, v.s_xo, kid0 - gap, kid1 + gap)
+
+        @pl.when(lev == 2)
+        def _():
+            to_slots(own, v.s_xo, i + 2)
+
         ssol[0] = sol
 
     @pl.when(host)
@@ -482,7 +558,11 @@
         drain(v.H5, v.r_h5)
         rs = (v.H5[0].astype(F32) - total(v.RX5, 16)).astype(BF16)
         v.SR5[b] = rs
-        drain(v.HM, v.r_hm)
+
+        @pl.when(x % 2 == 1)
+        def _():
+            drain(v.HM, v.r_hm)
+
         spread(v.TD, dot_t(rs, v.HM[...]))
         drain(v.HU.at[0], v.r_hu)
         v.TD[b] = (v.TD[b].astype(F32) + v.HU[0].astype(F32) + v.HU[1].astype(F32)).astype(BF16)
@@ -493,24 +573,33 @@
         others(lambda d, t: send(v.SR5.at[b], v.SR5.at[b], v.s_r5, v.r_r5, i, t))
         drain(v.SR5.at[pl.ds(0, 7)], v.r_r5)
         drain(v.HG5, v.r_hg5)
+
+        @pl.when(x % 2 == 0)
+        def _():
+            send(v.HG5, v.HG5, v.s_hr, v.r_hg5, near, b)
+
         v.Z5[...] = dot_t(full(v.SR5), v.HG5[...])
 
         drain(v.RX6.at[pl.ds(0, 15)], v.r_rx6)
         drain(v.H6, v.r_h6)
         v.SR6[b] = (v.H6[0].astype(F32) - total(v.RX6, 16)).astype(BF16)
         others(lambda d, t: send(v.SR6.at[b], v.SR6.at[b], v.s_r6, v.r_r6, i, t))
-        drain(v.HG6, v.r_hg6)
+
+        @pl.when(x != 1)
+        def _():
+            drain(v.HG6, v.r_hg6)
+
         drain(v.SR6.at[pl.ds(0, 7)], v.r_r6)
         sol6 = dot_t(full(v.SR6), v.HG6[...])
         v.XF[5, b] = sol6.astype(BF16)
         to_blk(5, v.s_xb.at[1])
-        to_kids(5, v.s_xf.at[5])
+        to_slots(5, v.s_xf.at[5], kid0, kid1)
         drain(v.XF.at[5, pl.ds(0, 7)], v.r_xf.at[5])
         x6 = full(v.XF.at[5])
         sol5 = v.Z5[...] - dot(x6, v.HM[...])
         v.XF[4, b] = sol5.astype(BF16)
         to_blk(4, v.s_xb.at[0])
-        to_kids(4, v.s_xf.at[4])
+        to_slots(4, v.s_xf.at[4], kid0, kid1)
         part = dot(x6, v.M[1])
 
         @pl.when(x == 1)
@@ -528,6 +617,7 @@
         v.SZ[...] = part + dot(full(v.XF.at[4]), v.M[0])
         finish()
         leaf_part(5)
+        leaf_product()
 
     for a in range(LEV, 1, -1):
         @pl.when((lev <= 3) & (lev < a))
@@ -535,13 +625,14 @@
             n = a - 1
             drain(v.XF.at[n], v.r_xf.at[n])
 
-            @pl.when(lev >= 2)
+            @pl.when((lev >= 2) & (a >= lev + 2))
             def _():
-                to_kids(n, v.s_xf.at[n])
-
-            @pl.when((lev == 1) & (a < lev_next))
-            def _():
-                to_pair(n, v.s_xf.at[n])
+                to_slots(n, v.s_xf.at[n], kid0, kid1)
+
+            if a >= 3:
+                @pl.when((lev == 1) & (a < lev_next))
+                def _():
+                    to_slots(n, v.s_xf.at[n], pair_slot)
 
             @pl.when(a >= lev + 3)
             def _():
@@ -562,7 +653,7 @@
 
             leaf_part(a)
 
-    @pl.when(normal)
+    @pl.when((lev >= 2) & normal)
     def _():
         drain(v.XF.at[lev - 1, pl.ds(0, 7)], v.r_xf.at[lev - 1])
         leaf_part(lev)
@@ -576,7 +667,7 @@
     def _():
         ssol[0] = jnp.zeros((64, 128), F32)
 
-    for a in range(LEV, 0, -1):
+    for a in range(LEV, 1, -1):
         @pl.when(a < lev)
         def _(a=a):
             drain(v.XF.at[a - 1], v.r_xf.at[a - 1])
@@ -584,8 +675,18 @@
 
     spread(v.LB, dot(v.LA[...].astype(BF16), v.li[0]))
     others(lambda d, t: send(v.LB.at[t], v.RLB.at[d - 1], v.s_lb, v.r_lb, i, t))
+
+    @pl.when(lev == 1)
+    def _():
+        drain(v.XF.at[0, pl.ds(0, 7)], v.r_xf.at[0])
+
+    @pl.when(lev != 1)
+    def _():
+        drain(v.XF.at[0], v.r_xf.at[0])
+
+    last = pat[0, 0].astype(F32) * dot(full(v.XF.at[0]), v.ML[...])
     drain(v.RLB, v.r_lb)
-    lsol[0] = v.LB[b].astype(F32) + total(v.RLB, 7)
+    lsol[0] = v.LB[b].astype(F32) + total(v.RLB, 7) - last
 
     seven = pl.ds(0, 7)
     drain(v.LR.at[seven], v.s_lr)
@@ -603,18 +704,24 @@
     for n in range(LEV - 1):
         drain(v.TL.at[n, seven], v.s_tl.at[n])
     drain(v.LB.at[seven], v.s_lb)
+    drain(v.IL.at[seven], v.s_ig.at[1])
+    drain(v.CL.at[seven], v.s_g.at[3])
 
     @pl.when(normal)
     def _():
         drain(v.SR.at[seven], v.s_sr)
         drain(v.RX.at[pl.ds(0, 14)], v.s_pb)
-        drain(v.IG.at[seven], v.s_ig)
+        drain(v.IG.at[seven], v.s_ig.at[0])
         drain(v.CG.at[0, seven], v.s_g.at[0])
         drain(v.CG.at[1, seven], v.s_g.at[1])
 
-        @pl.when(lev >= 2)
-        def _():
-            drain(v.RX, v.s_xo)
+        @pl.when(lev >= 3)
+        def _():
+            drain(v.XF, v.s_xo)
+
+        @pl.when(lev == 2)
+        def _():
+            drain(v.XF.at[pl.ds(0, 3)], v.s_xo)
 
         @pl.when(lev == 1)
         def _():
@@ -646,21 +753,30 @@
 
     @pl.when(own5 | own6)
     def _():
-        drain(v.IG.at[seven], v.s_ig)
+        drain(v.IG.at[seven], v.s_ig.at[0])
         drain(v.VG.at[seven], v.s_g.at[2])
-        drain(v.CG.at[0, pl.ds(0, 4)], v.s_hm)
 
     @pl.when(own5)
     def _():
+        drain(v.CG.at[0, pl.ds(0, 2)], v.s_hm)
         drain(v.CG.at[0, seven], v.s_g.at[0])
         drain(v.PB.at[pl.ds(0, 2)], v.s_hs)
 
     @pl.when(own6)
     def _():
+        drain(v.CG.at[0, 0], v.s_hm)
         drain(v.PB.at[pl.ds(0, 4)], v.s_hs)
 
-    for a in range(LEV, 1, -1):
-        @pl.when((lev < a) & ((lev == 2) | (lev == 3)))
+    @pl.when(host & (x % 2 == 0))
+    def _():
+        drain(v.CG.at[0, pl.ds(0, 2)], v.s_hr)
+
+    @pl.when(host & (x == 1))
+    def _():
+        drain(v.CG.at[0, pl.ds(0, 3)], v.s_hr)
+
+    for a in range(LEV, 2, -1):
+        @pl.when((lev + 2 <= a) & ((lev == 2) | (lev == 3)))
         def _(a=a):
             drain(v.RX, v.s_xf.at[a - 1])
 

time: 155 us -> 144 us (0.929)
  the two profiles are of different devices: /device:TPU:1 before, /device:TPU:3 now
where the time goes in v4:
time: 144 us; the launch traced here: 143 us
  Pallas kernels  140 us (97%)
  local copies, waits for them, and re-layouts  2.75 us (2%)
    pallas_call x1, Pallas kernels, body(): pl.pallas_call(kernel, out_shape=(out, out), in_specs=[pl.BlockSpec(memor...  140 us

profile of v4, /device:TPU:3, one launch (start us, length us, event | category | flops | bytes accessed | tf_op | source)
XLA Modules:
  0.0 143.3 jit_solution(16735520907378206546)
XLA Ops:
  0.6 139.9 %solve.1 = (f32[1,64,128]{2,1,0:T(8,128)}, f32[1,64,128]{2,1,0:T(8,128)}) custom-call(bf16[1,128,1024]{2,1,0:T(8,128)(2,1)} %li_in.1, bf16[1,6,1024,128]{3,2,1,0:T(8,128)(2,1)} %lc_in.1, bf16[1,128,1024]{2,1,0:T(8,128)(2,1)} %si_in.1, bf16[1,6,1024,128]{3,2,1,0:T(8,128)(2,1)} %sc_in.1, bf16[1,64,128]{2,1,0:T(8,128)(2,1)} %lr_in.1, ...), custom_call_target="tpu_custom_call" | custom-call | tf_op jit(solution)/shard_map/solve/pallas_call | solution.py:791
  140.5 1.4 copy.11
  141.9 1.4 copy.12

commit v5 on v4

--- a/solution.py
+++ b/solution.py
@@ -61,9 +61,9 @@
     IG=blocks(8, 128, 128), CG=blocks(2, 8, 1024, 128), VG=blocks(8, 128, 1024), M=blocks(2, 1024, 128), G=blocks(128, 1024),
     CL=blocks(8, 1024, 128), IL=blocks(8, 128, 128), ML=blocks(1024, 128),
     s_ig=sems(2), r_ig=sems(2), l_ig=sems(2), s_g=sems(4), ru_g=sems(4), rd_g=sems(4), rf_g=sems(4), rm_g=sems(4), l_g=sems(4),
-    HM=blocks(1024, 128), HG5=blocks(128, 1024), HG6=blocks(128, 1024), H5=chunks(1), H6=chunks(1),
-    s_hm=sems(), s_hr=sems(), s_hs=sems(), r_hm=sems(), r_hg5=sems(), r_hg6=sems(), r_h5=sems(), r_h6=sems(),
-    RX5=chunks(16), RX6=chunks(16), SR5=chunks(8), SR6=chunks(8), TD=chunks(8), HU=chunks(2), Z5=chunks(dtype=F32),
+    HM=blocks(1024, 128), HI5=blocks(1, 128, 1024), HG6=blocks(128, 1024), H5=chunks(1), H6=chunks(1),
+    s_hm=sems(), s_hr=sems(), s_hs=sems(), r_hm=sems(), r_hi5=sems(), r_hg6=sems(), r_h5=sems(), r_h6=sems(),
+    RX5=chunks(16), RX6=chunks(16), SR5=chunks(8), SR6=chunks(8), TD=chunks(8), HU=chunks(2), PB5=chunks(8), RSB5=chunks(7), s_p5=sems(), r_p5=sems(),
     r_rx5=sems(), r_rx6=sems(), s_r5=sems(), r_r5=sems(), s_r6=sems(), r_r6=sems(), s_td=sems(), r_hu=sems(),
     HX=chunks(dtype=F32), HY=chunks(dtype=F32), s_hx=sems(), r_hx=sems(),
     LB=chunks(8), RLB=chunks(7), s_lb=sems(), r_lb=sems(),
@@ -106,15 +106,19 @@
     def drain(ref, sem):
         pltpu.make_async_copy(ref, ref, sem).wait()
 
+    def offset(k):
+        return 4 + ((k + 1) // 2) * (2 * (k % 2) - 1)
+
     def others(fn):
-        def step(d, c):
+        def step(k, c):
+            d = offset(k)
             fn(d, (b + d) % NB)
             return c
-        lax.fori_loop(1, NB, step, 0)
+        lax.fori_loop(0, NB - 1, step, 0)
 
     def all_blk(fn):
-        def step(d, c):
-            fn((b + d) % NB)
+        def step(k, c):
+            fn((b + offset(k)) % NB)
             return c
         lax.fori_loop(0, NB, step, 0)
 
@@ -335,6 +339,7 @@
         @pl.when(own5)
         def _():
             gather_start(0, v.sc.at[0, 5], v.CG.at[0])
+            send(v.si, v.HI5, v.s_hm, v.r_hi5, host_a, b)
 
         @pl.when(own6)
         def _():
@@ -363,6 +368,8 @@
 
         @pl.when(host & (x % 2 == 0))
         def _():
+            drain(v.HI5, v.r_hi5)
+            send(v.HI5, v.HI5, v.s_hr, v.r_hi5, near, b)
             drain(v.HM, v.r_hm)
             send(v.HM, v.HM, v.s_hr, v.r_hm, near, b)
 
@@ -377,7 +384,6 @@
         @pl.when(own5)
         def _():
             gather_relay(0, v.CG.at[0])
-            gather_start(2, v.si.at[0], v.VG)
 
         @pl.when(own6)
         def _():
@@ -390,17 +396,11 @@
             gather_end(0, v.CG.at[0])
             form_m(v.M.at[0], v.CG.at[0], v.IG)
             send(v.M.at[0], v.HM, v.s_hm, v.r_hm, host_a, b)
-            gather_relay(2, v.VG)
-
-        gather_end(2, v.VG)
-        form_g()
-
-        @pl.when(own5)
-        def _():
-            send(v.G, v.HG5, v.s_hm, v.r_hg5, host_a, b)
 
         @pl.when(own6)
         def _():
+            gather_end(2, v.VG)
+            form_g()
             send(v.G, v.HG6, v.s_hm, v.r_hg6, 23, b)
 
     @pl.when(z == 15)
@@ -572,13 +572,14 @@
         others(lambda d, t: send(v.TD.at[t], v.RX6.at[mine], v.s_td, v.r_rx6, i, t))
         others(lambda d, t: send(v.SR5.at[b], v.SR5.at[b], v.s_r5, v.r_r5, i, t))
         drain(v.SR5.at[pl.ds(0, 7)], v.r_r5)
-        drain(v.HG5, v.r_hg5)
-
-        @pl.when(x % 2 == 0)
-        def _():
-            send(v.HG5, v.HG5, v.s_hr, v.r_hg5, near, b)
-
-        v.Z5[...] = dot_t(full(v.SR5), v.HG5[...])
+
+        @pl.when(x % 2 == 1)
+        def _():
+            drain(v.HI5, v.r_hi5)
+
+        sy5 = dot_t(full(v.SR5), v.HI5[0])
+        spread(v.PB5, dot(sy5.astype(BF16), v.HI5[0]))
+        others(lambda d, t: send(v.PB5.at[t], v.RSB5.at[d - 1], v.s_p5, v.r_p5, i, t))
 
         drain(v.RX6.at[pl.ds(0, 15)], v.r_rx6)
         drain(v.H6, v.r_h6)
@@ -596,7 +597,8 @@
         to_slots(5, v.s_xf.at[5], kid0, kid1)
         drain(v.XF.at[5, pl.ds(0, 7)], v.r_xf.at[5])
         x6 = full(v.XF.at[5])
-        sol5 = v.Z5[...] - dot(x6, v.HM[...])
+        drain(v.RSB5, v.r_p5)
+        sol5 = v.PB5[b].astype(F32) + total(v.RSB5, 7) - dot(x6, v.HM[...])
         v.XF[4, b] = sol5.astype(BF16)
         to_blk(4, v.s_xb.at[0])
         to_slots(4, v.s_xf.at[4], kid0, kid1)
@@ -751,10 +753,13 @@
         def _():
             drain(v.HX, v.s_hx)
 
+    @pl.when(host)
+    def _():
+        drain(v.PB5.at[seven], v.s_p5)
+
     @pl.when(own5 | own6)
     def _():
         drain(v.IG.at[seven], v.s_ig.at[0])
-        drain(v.VG.at[seven], v.s_g.at[2])
 
     @pl.when(own5)
     def _():
@@ -765,6 +770,7 @@
     @pl.when(own6)
     def _():
         drain(v.CG.at[0, 0], v.s_hm)
+        drain(v.VG.at[seven], v.s_g.at[2])
         drain(v.PB.at[pl.ds(0, 4)], v.s_hs)
 
     @pl.when(host & (x % 2 == 0))

time: 144 us -> 136 us (0.944)
  the two profiles are of different devices: /device:TPU:3 before, /device:TPU:1 now
where the time goes in v5:
time: 136 us
  Pallas kernels  132 us (97%)
  local copies, waits for them, and re-layouts  2.75 us (2%)
    pallas_call x1, Pallas kernels, body(): pl.pallas_call(kernel, out_shape=(out, out), in_specs=[pl.BlockSpec(memor...  132 us
    unnamed x2, local copies, waits for them, and re-layouts  2.75 us

profile of v5, /device:TPU:1, one launch (start us, length us, event | category | flops | bytes accessed | tf_op | source)
XLA Modules:
  0.0 135.6 jit_solution(9685898815037508917)
XLA Ops:
  0.6 132.2 %solve.1 = (f32[1,64,128]{2,1,0:T(8,128)}, f32[1,64,128]{2,1,0:T(8,128)}) custom-call(bf16[1,128,1024]{2,1,0:T(8,128)(2,1)} %li_in.1, bf16[1,6,1024,128]{3,2,1,0:T(8,128)(2,1)} %lc_in.1, bf16[1,128,1024]{2,1,0:T(8,128)(2,1)} %si_in.1, bf16[1,6,1024,128]{3,2,1,0:T(8,128)(2,1)} %sc_in.1, bf16[1,64,128]{2,1,0:T(8,128)(2,1)} %lr_in.1, ...), custom_call_target="tpu_custom_call" | custom-call | tf_op jit(solution)/shard_map/solve/pallas_call | solution.py:797
  132.9 1.4 %copy.11 = f32[1,64,128]{2,1,0:T(8,128)} copy(f32[1,64,128]{2,1,0:T(8,128)} %get-tuple-element.4) | data formatting | bytes 65536
  134.2 1.4 %copy.12 = f32[1,64,128]{2,1,0:T(8,128)} copy(f32[1,64,128]{2,1,0:T(8,128)} %get-tuple-element.5) | data formatting | bytes 65536

commit v6 on v5

--- a/solution.py
+++ b/solution.py
@@ -418,8 +418,11 @@
 
         return v.U[n] + v.UX[n, 0].astype(F32) + v.UX[n, 1].astype(F32)
 
-    def to_parent(n):
+    def to_parent_start(value):
+        spread(v.TC, value)
         others(lambda d, t: send(v.TC.at[t], v.RX.at[side * NB + b], v.s_tc, v.r_rx, parent, t))
+
+    def to_parent_end(n):
         v.TC[b] = (v.TC[b].astype(F32) + upward(n)).astype(BF16)
         send(v.TC.at[b], v.RX.at[side * NB + b], v.s_tc, v.r_rx, parent, b)
 
@@ -447,23 +450,32 @@
 
         @pl.when(early)
         def _():
-            spread(v.TC, dot_t(rsb, v.M[0]))
-
             @pl.when(lev == 3)
             def _():
-                to_parent(2)
+                to_parent_start(dot_t(rsb, v.M[0]))
                 over_blk(5, dot_t(rsb, v.M[1]))
 
             @pl.when(lev == 4)
             def _():
-                v.TC[b] = (v.TC[b].astype(F32) + upward(3)).astype(BF16)
+                spread(v.TC, dot_t(rsb, v.M[0]))
                 mine = (x % 2) * NB + b
-                v.RX5[mine] = v.TC[b]
-                all_blk(lambda t: send(v.TC.at[t], v.RX5.at[mine], v.s_tc, v.r_rx5, near, t))
+                others(lambda d, t: send(v.TC.at[t], v.RX5.at[mine], v.s_tc, v.r_rx5, near, t))
                 others(lambda d, t: send(v.TC.at[t], v.RX5.at[mine], v.s_tc, v.r_rx5, i, t))
                 over_blk(6, dot_t(rsb, v.M[1]))
 
         others(lambda d, t: send(v.SR.at[b], v.SR.at[b], v.s_sr, v.r_sr, i, t))
+
+        @pl.when(lev == 3)
+        def _():
+            to_parent_end(2)
+
+        @pl.when(lev == 4)
+        def _():
+            v.TC[b] = (v.TC[b].astype(F32) + upward(3)).astype(BF16)
+            mine = (x % 2) * NB + b
+            v.RX5[mine] = v.TC[b]
+            send(v.TC.at[b], v.RX5.at[mine], v.s_tc, v.r_rx5, near, b)
+
         drain(v.SR.at[pl.ds(0, 7)], v.r_sr)
         sy = dot_t(full(v.SR), v.si[0])
         v.SA[...] = sy
@@ -472,13 +484,22 @@
         for a in (2, 3):
             @pl.when(lev == a - 1)
             def _(a=a):
-                spread(v.TC, dot_t(syb, v.sc[0, a - 1]))
-                to_parent(a - 2)
+                to_parent_start(dot_t(syb, v.sc[0, a - 1]))
 
         for a in range(3, LEV + 1):
             @pl.when((lev < a - 1) & ((lev <= 2) | ((lev == 3) & (a == 6))))
             def _(a=a):
                 over_blk(a, dot_t(syb, v.sc[0, a - 1]))
+
+            if a == 3:
+                @pl.when(lev == 1)
+                def _():
+                    to_parent_end(0)
+
+            if a == 4:
+                @pl.when(lev == 2)
+                def _():
+                    to_parent_end(1)
 
         for a in range(3, LEV + 1):
             n = a - 2

time: 136 us -> 132 us (0.971)
  Pallas kernels: 132 us -> 128 us
    pallas_call x1, Pallas kernels: 132 us -> 128 us  [body(): pl.pallas_call(kernel, out_shape=(out, out), in_specs=[pl.BlockSpec(memor...]
where the time goes in v6:
time: 132 us
  Pallas kernels  128 us (97%)
  local copies, waits for them, and re-layouts  2.75 us (2%)
    pallas_call x1, Pallas kernels, body(): pl.pallas_call(kernel, out_shape=(out, out), in_specs=[pl.BlockSpec(memor...  128 us
    unnamed x2, local copies, waits for them, and re-layouts  2.75 us

profile of v6, /device:TPU:1, one launch (start us, length us, event | category | flops | bytes accessed | tf_op | source)
XLA Modules:
  0.0 131.6 jit_solution(3738600484562053021)
XLA Ops:
  0.6 128.2 %solve.1 = (f32[1,64,128]{2,1,0:T(8,128)}, f32[1,64,128]{2,1,0:T(8,128)}) custom-call(bf16[1,128,1024]{2,1,0:T(8,128)(2,1)} %li_in.1, bf16[1,6,1024,128]{3,2,1,0:T(8,128)(2,1)} %lc_in.1, bf16[1,128,1024]{2,1,0:T(8,128)(2,1)} %si_in.1, bf16[1,6,1024,128]{3,2,1,0:T(8,128)(2,1)} %sc_in.1, bf16[1,64,128]{2,1,0:T(8,128)(2,1)} %lr_in.1, ...), custom_call_target="tpu_custom_call" | custom-call | tf_op jit(solution)/shard_map/solve/pallas_call | solution.py:818
  128.9 1.4 %copy.11 = f32[1,64,128]{2,1,0:T(8,128)} copy(f32[1,64,128]{2,1,0:T(8,128)} %get-tuple-element.4) | data formatting | bytes 65536
  130.3 1.4 %copy.12 = f32[1,64,128]{2,1,0:T(8,128)} copy(f32[1,64,128]{2,1,0:T(8,128)} %get-tuple-element.5) | data formatting | bytes 65536

commit v7 on v6

--- a/solution.py
+++ b/solution.py
@@ -63,7 +63,7 @@
     s_ig=sems(2), r_ig=sems(2), l_ig=sems(2), s_g=sems(4), ru_g=sems(4), rd_g=sems(4), rf_g=sems(4), rm_g=sems(4), l_g=sems(4),
     HM=blocks(1024, 128), HI5=blocks(1, 128, 1024), HG6=blocks(128, 1024), H5=chunks(1), H6=chunks(1),
     s_hm=sems(), s_hr=sems(), s_hs=sems(), r_hm=sems(), r_hi5=sems(), r_hg6=sems(), r_h5=sems(), r_h6=sems(),
-    RX5=chunks(16), RX6=chunks(16), SR5=chunks(8), SR6=chunks(8), TD=chunks(8), HU=chunks(2), PB5=chunks(8), RSB5=chunks(7), s_p5=sems(), r_p5=sems(),
+    RX5=chunks(16), RX6=chunks(16), SR5=chunks(8), SR6=chunks(8), TD=chunks(8), HU=chunks(4), PB5=chunks(8), RSB5=chunks(7), s_p5=sems(), r_p5=sems(),
     r_rx5=sems(), r_rx6=sems(), s_r5=sems(), r_r5=sems(), s_r6=sems(), r_r6=sems(), s_td=sems(), r_hu=sems(),
     HX=chunks(dtype=F32), HY=chunks(dtype=F32), s_hx=sems(), r_hx=sems(),
     LB=chunks(8), RLB=chunks(7), s_lb=sems(), r_lb=sems(),
@@ -95,6 +95,7 @@
     x_far = (x + 2) % 4
     near = x_near * 16 + 7
     far = x_far * 16 + 7
+    cross = (3 - x) * 16 + 7
     host_a = (x - x % 2) * 16 + 7
     host_b = host_a + 16
     owner5 = (x - x % 2) * 16 + 15
@@ -162,6 +163,7 @@
         greet(31, b)
         greet(near, b)
         greet(far, b)
+        greet(cross, b)
 
     @pl.when(own5)
     def _():
@@ -211,7 +213,7 @@
     peers = (7 + jnp.where(pair_is_kin, 0, 1) + jnp.where(lev <= 3, 1, 0) + jnp.where(lev <= 2, 1, 0)
              + jnp.where((z == 13) | (z == 15), 1, 0)
              + jnp.where(has_kids, 2, 0) + jnp.where(has_grandkids, 4, 0)
-             + jnp.where(host, 4, 0) + jnp.where(own5, 2, 0) + jnp.where(own6, 4, 0))
+             + jnp.where(host, 5, 0) + jnp.where(own5, 2, 0) + jnp.where(own6, 4, 0))
     pl.semaphore_wait(barrier, peers)
 
     up, down = (b + 2) % NB, (b + 6) % NB
@@ -308,6 +310,23 @@
         for h in range(4):
             send(v.SRI, v.H6, v.s_hs, v.r_h6, 16 * h + 7, b)
 
+    @pl.when(own5 | own6)
+    def _():
+        columns_start(0, v.si, v.IG)
+
+        @pl.when(own5)
+        def _():
+            gather_start(0, v.sc.at[0, 5], v.CG.at[0])
+            send(v.si, v.HI5, v.s_hm, v.r_hi5, host_a, b)
+
+        @pl.when(own6)
+        def _():
+            gather_start(2, v.si.at[0], v.VG)
+
+    @pl.when(early)
+    def _():
+        products_start0()
+
     drain(v.LR.at[pl.ds(0, 7)], v.r_lr)
     ly = dot_t(full(v.LR), v.li[0])
     v.LA[...] = ly
@@ -328,22 +347,17 @@
         spread(v.TL.at[n], dot_t(lyb, v.lc[0, a - 1]) * pat[0, a - 1].astype(F32))
         others(lambda d, t, n=n: send(v.TL.at[n, t], v.RSL.at[n, d - 1], v.s_tl.at[n], v.r_tl.at[n], i, t))
 
+    @pl.when(own5)
+    def _():
+        gather_relay(0, v.CG.at[0])
+
+    @pl.when(own6)
+    def _():
+        gather_relay(2, v.VG)
+
     @pl.when(early)
     def _():
-        products_start0()
-
-    @pl.when(own5 | own6)
-    def _():
-        columns_start(0, v.si, v.IG)
-
-        @pl.when(own5)
-        def _():
-            gather_start(0, v.sc.at[0, 5], v.CG.at[0])
-            send(v.si, v.HI5, v.s_hm, v.r_hi5, host_a, b)
-
-        @pl.when(own6)
-        def _():
-            gather_start(2, v.si.at[0], v.VG)
+        products_start1()
 
     for a in range(2, LEV + 1):
         n = a - 2
@@ -363,7 +377,6 @@
 
     @pl.when(early)
     def _():
-        products_start1()
         products_end()
 
         @pl.when(host & (x % 2 == 0))
@@ -381,14 +394,6 @@
 
     @pl.when(own5 | own6)
     def _():
-        @pl.when(own5)
-        def _():
-            gather_relay(0, v.CG.at[0])
-
-        @pl.when(own6)
-        def _():
-            gather_relay(2, v.VG)
-
         columns_end(0, v.IG)
 
         @pl.when(own5)
@@ -504,21 +509,12 @@
         for a in range(3, LEV + 1):
             n = a - 2
 
-            @pl.when(lev < a - 1)
+            @pl.when((lev < a - 1) & (lev <= 3))
             def _(a=a, n=n):
                 drain(v.RSS.at[a - 3], v.r_tn.at[a - 3])
                 acc = v.TN[a - 3, b].astype(F32) + total(v.RSS.at[a - 3], 7) + upward(n)
                 v.UO2[n] = acc.astype(BF16)
-
-                @pl.when(lev <= 3)
-                def _():
-                    send(v.UO2.at[n], v.UX.at[n, side], v.s_u2.at[n], v.r_ux.at[n], parent, b)
-
-                if a == 6:
-                    @pl.when(lev == 4)
-                    def _():
-                        v.HU[x % 2] = v.UO2[n]
-                        send(v.UO2.at[n], v.HU.at[x % 2], v.s_u2.at[n], v.r_hu, near, b)
+                send(v.UO2.at[n], v.UX.at[n, side], v.s_u2.at[n], v.r_ux.at[n], parent, b)
 
         @pl.when(lev == 4)
         def _():
@@ -585,13 +581,19 @@
             drain(v.HM, v.r_hm)
 
         spread(v.TD, dot_t(rs, v.HM[...]))
-        drain(v.HU.at[0], v.r_hu)
-        v.TD[b] = (v.TD[b].astype(F32) + v.HU[0].astype(F32) + v.HU[1].astype(F32)).astype(BF16)
         mine = (x // 2) * NB + b
         v.RX6[mine] = v.TD[b]
         all_blk(lambda t: send(v.TD.at[t], v.RX6.at[mine], v.s_td, v.r_rx6, far, t))
         others(lambda d, t: send(v.TD.at[t], v.RX6.at[mine], v.s_td, v.r_rx6, i, t))
         others(lambda d, t: send(v.SR5.at[b], v.SR5.at[b], v.s_r5, v.r_r5, i, t))
+
+        drain(v.RSS.at[3], v.r_tn.at[3])
+        acc = v.TN[3, b].astype(F32) + total(v.RSS.at[3], 7) + upward(4)
+        v.UO2[4] = acc.astype(BF16)
+        v.HU[x] = v.UO2[4]
+        for slot in (near, far, cross):
+            send(v.UO2.at[4], v.HU.at[x], v.s_u2.at[4], v.r_hu, slot, b)
+
         drain(v.SR5.at[pl.ds(0, 7)], v.r_r5)
 
         @pl.when(x % 2 == 1)
@@ -604,7 +606,8 @@
 
         drain(v.RX6.at[pl.ds(0, 15)], v.r_rx6)
         drain(v.H6, v.r_h6)
-        v.SR6[b] = (v.H6[0].astype(F32) - total(v.RX6, 16)).astype(BF16)
+        drain(v.HU.at[pl.ds(0, 3)], v.r_hu)
+        v.SR6[b] = (v.H6[0].astype(F32) - total(v.RX6, 16) - total(v.HU, 4)).astype(BF16)
         others(lambda d, t: send(v.SR6.at[b], v.SR6.at[b], v.s_r6, v.r_r6, i, t))
 
         @pl.when(x != 1)
@@ -758,10 +761,14 @@
             @pl.when(lev < a - 1)
             def _(a=a):
                 drain(v.TN.at[a - 3, seven], v.s_tn.at[a - 3])
+
+            @pl.when((lev < a - 1) & (lev <= 3))
+            def _(a=a):
                 drain(v.UO2.at[a - 2], v.s_u2.at[a - 2])
 
     @pl.when(host)
     def _():
+        drain(v.UO2.at[pl.ds(0, 3)], v.s_u2.at[4])
         drain(v.RX.at[pl.ds(0, 15)], v.s_tc)
         drain(v.RX.at[pl.ds(0, 15)], v.s_td)
         drain(v.SR5.at[seven], v.s_r5)

time: 132 us -> 129 us (0.977)
  the two profiles are of different devices: /device:TPU:1 before, /device:TPU:484 now
where the time goes in v7:
time: 129 us
  Pallas kernels  125 us (97%)
  local copies, waits for them, and re-layouts  2.75 us (2%)
    pallas_call x1, Pallas kernels, body(): pl.pallas_call(kernel, out_shape=(out, out), in_specs=[pl.BlockSpec(memor...  125 us
    unnamed x2, local copies, waits for them, and re-layouts  2.75 us

profile of v7, /device:TPU:484, one launch (start us, length us, event | category | flops | bytes accessed | tf_op | source)
XLA Modules:
  0.0 128.7 jit_solution(5881881756083018587)
XLA Ops:
  0.6 125.3 %solve.1 = (f32[1,64,128]{2,1,0:T(8,128)}, f32[1,64,128]{2,1,0:T(8,128)}) custom-call(bf16[1,128,1024]{2,1,0:T(8,128)(2,1)} %li_in.1, bf16[1,6,1024,128]{3,2,1,0:T(8,128)(2,1)} %lc_in.1, bf16[1,128,1024]{2,1,0:T(8,128)(2,1)} %si_in.1, bf16[1,6,1024,128]{3,2,1,0:T(8,128)(2,1)} %sc_in.1, bf16[1,64,128]{2,1,0:T(8,128)(2,1)} %lr_in.1, ...), custom_call_target="tpu_custom_call" | custom-call | tf_op jit(solution)/shard_map/solve/pallas_call | solution.py:825
  125.9 1.4 %copy.11 = f32[1,64,128]{2,1,0:T(8,128)} copy(f32[1,64,128]{2,1,0:T(8,128)} %get-tuple-element.4) | data formatting | bytes 65536
  127.3 1.4 %copy.12 = f32[1,64,128]{2,1,0:T(8,128)} copy(f32[1,64,128]{2,1,0:T(8,128)} %get-tuple-element.5) | data formatting | bytes 65536

commit v8 on v7

--- a/solution.py
+++ b/solution.py
@@ -111,17 +111,12 @@
         return 4 + ((k + 1) // 2) * (2 * (k % 2) - 1)
 
     def others(fn):
-        def step(k, c):
-            d = offset(k)
-            fn(d, (b + d) % NB)
-            return c
-        lax.fori_loop(0, NB - 1, step, 0)
+        for k in range(NB - 1):
+            fn(offset(k), (b + offset(k)) % NB)
 
     def all_blk(fn):
-        def step(k, c):
+        for k in range(NB):
             fn((b + offset(k)) % NB)
-            return c
-        lax.fori_loop(0, NB, step, 0)
 
     def full(ref):
         return jnp.concatenate([ref[c] for c in range(NB)], axis=1)

time: 129 us -> 129 us (level)
  no operation moved by 1% of the time
where the time goes in v8:
time: 129 us; the launch traced here: 128 us
  Pallas kernels  125 us (97%)
  local copies, waits for them, and re-layouts  2.75 us (2%)
    pallas_call x1, Pallas kernels, body(): pl.pallas_call(kernel, out_shape=(out, out), in_specs=[pl.BlockSpec(memor...  125 us
    unnamed x2, local copies, waits for them, and re-layouts  2.75 us

profile of v8, /device:TPU:484, one launch (start us, length us, event | category | flops | bytes accessed | tf_op | source)
XLA Modules:
  0.0 128.3 jit_solution(10017964064445173092)
XLA Ops:
  0.6 124.9 %solve.1 = (f32[1,64,128]{2,1,0:T(8,128)}, f32[1,64,128]{2,1,0:T(8,128)}) custom-call(bf16[1,128,1024]{2,1,0:T(8,128)(2,1)} %li_in.1, bf16[1,6,1024,128]{3,2,1,0:T(8,128)(2,1)} %lc_in.1, bf16[1,128,1024]{2,1,0:T(8,128)(2,1)} %si_in.1, bf16[1,6,1024,128]{3,2,1,0:T(8,128)(2,1)} %sc_in.1, bf16[1,64,128]{2,1,0:T(8,128)(2,1)} %lr_in.1, ...), custom_call_target="tpu_custom_call" | custom-call | tf_op jit(solution)/shard_map/solve/pallas_call | solution.py:820
  125.6 1.4 %copy.11 = f32[1,64,128]{2,1,0:T(8,128)} copy(f32[1,64,128]{2,1,0:T(8,128)} %get-tuple-element.4) | data formatting | bytes 65536
  127.0 1.4 %copy.12 = f32[1,64,128]{2,1,0:T(8,128)} copy(f32[1,64,128]{2,1,0:T(8,128)} %get-tuple-element.5) | data formatting | bytes 65536
